TPU v7x, 512 devices: a whole 4x4x16 slice. The times are simulated.
512 devices in a mesh: grp: 32 (over z_lo, y, core), sub: 16 (over z_hi, x).
Axes of the slice: x: 4, y: 4, z: 16 (z_hi: 4, z_lo: 4; z = z_hi * 4 + z_lo), core: 2. Of those that a mesh axis runs over, the one named last changes fastest.
Arguments:
- coeffs: bfloat16 [64, 240, 8192], P('grp', None, 'sub'), may hold values from -0.0625 to 0.0625
- offsets: bfloat16 [64, 3, 8192], P('grp', None, 'sub'), may hold values from -6 to 6
- moments: bfloat16 [64, 3, 8192], P('grp', None, 'sub'), may hold values from -6 to 6
- centers: float32 [64, 3], replicated, may hold values from -40 to 40
- near_flags: int32 [64, 64], replicated, may hold values from 0 to 1, as said below
- lobe_weights: float32 [1440], P('sub'), may hold values from 0.3 to 3
- near_boost: float32 [1440], P('sub'), may hold values from 0.5 to 2
Outputs:
- lower_coupling: float32 [64, 2, 2, 240, 240], P('grp', None, None, None, 'sub')
- upper_coupling: float32 [64, 2, 2, 240, 240], P('grp', None, None, 'sub')
Inputs may be any that keep to these rules, and one draw needn't show every extreme that they name: near_flags is symmetric: near_flags[m, n] equals near_flags[n, m].
All inputs are finite; a program needn't handle non-finite values.
Results may differ from a plain program's by a relative error of at most 0.02.
Values may be sent and summed in bfloat16 or wider, within the bound.
A program may use at most 64 MiB of HBM per device.

v0:
```python
import math

import jax
import jax.numpy as jnp
from jax import lax
from jax.sharding import PartitionSpec as P

THETAS = 20
PHIS = 36
DIRS = 720
LOBE_TOTAL = 1440
ROUND_TOTAL = 2


wave_number = math.pi
highest = lax.Precision.HIGHEST


def shifted(value, axis, steps):
    count = lax.axis_size(axis)
    pairs = [(source, (source + steps) % count) for source in range(count)]
    return lax.ppermute(value, axis, pairs)


def lobe_vectors(lobe_ids):
    polar = lobe_ids // DIRS
    place = lobe_ids % DIRS
    theta = math.pi * ((place // PHIS).astype(jnp.float32) + 0.5) / THETAS
    azimuth = 2.0 * math.pi * (place % PHIS).astype(jnp.float32) / PHIS
    sin_theta = jnp.sin(theta)
    cos_theta = jnp.cos(theta)
    sin_azimuth = jnp.sin(azimuth)
    cos_azimuth = jnp.cos(azimuth)
    heading = jnp.stack([sin_theta * cos_azimuth, sin_theta * sin_azimuth, cos_theta])
    along_theta = jnp.stack([cos_theta * cos_azimuth, cos_theta * sin_azimuth, -sin_theta])
    along_phi = jnp.stack([-sin_azimuth, cos_azimuth, jnp.zeros_like(sin_azimuth)])
    field = jnp.where((polar == 0)[None, :], along_theta, along_phi)
    return (heading, field)


def samples(heading, field, offsets, moments):
    phase = wave_number * jnp.einsum(
        "cl,bcu->blu", heading, offsets.astype(jnp.float32), precision=highest
    )
    weight = jnp.einsum("cl,bcu->blu", field, moments.astype(jnp.float32), precision=highest)
    return jnp.stack([weight * jnp.cos(phase), -weight * jnp.sin(phase)], axis=1).astype(
        jnp.bfloat16
    )


def couple(mine, theirs, mine_centers, their_centers, flags, heading, weights, boost):
    along_mine = jnp.einsum("ic,cl->il", mine_centers, heading, precision=highest)
    along_theirs = jnp.einsum("jc,cl->jl", their_centers, heading, precision=highest)
    angle = wave_number * (along_mine[:, None, :] - along_theirs[None, :, :])
    amplitude = (
        weights[None, None, :] + flags[:, :, None].astype(jnp.float32) * boost[None, None, :]
    ) / math.sqrt(LOBE_TOTAL)
    cosine = (amplitude * jnp.cos(angle))[..., None]
    sine = (amplitude * jnp.sin(angle))[..., None]
    right = theirs.astype(jnp.float32)
    real_part = right[:, 0][None]
    imag_part = right[:, 1][None]
    carry_real = (cosine * real_part - sine * imag_part).astype(jnp.bfloat16)
    carry_imag = (sine * real_part + cosine * imag_part).astype(jnp.bfloat16)
    first = jnp.einsum("ila,ijlb->ijab", mine[:, 0], carry_real, preferred_element_type=jnp.float32)
    second = jnp.einsum(
        "ila,ijlb->ijab", mine[:, 1], carry_imag, preferred_element_type=jnp.float32
    )
    return first + second


def shards(coeffs, offsets, moments, centers, near_flags, lobe_weights, near_boost):
    group_blocks = coeffs.shape[0]
    lobe_count = lobe_weights.shape[0]
    group_count = lax.axis_size("grp")
    group_index = lax.axis_index("grp")
    sub_index = lax.axis_index("sub")
    lobe_ids = sub_index * lobe_count + jnp.arange(lobe_count, dtype=jnp.int32)
    heading, field = lobe_vectors(lobe_ids)
    coeff_piece = lax.all_gather(coeffs, "sub", axis=2, tiled=True)
    offset_piece = lax.all_gather(offsets, "sub", axis=2, tiled=True)
    moment_piece = lax.all_gather(moments, "sub", axis=2, tiled=True)
    sample_draw = samples(heading, field, offset_piece, moment_piece)
    lobe_totals = jnp.einsum(
        "bclu,bku->bclk", sample_draw, coeff_piece, preferred_element_type=jnp.float32
    )
    wave_patterns = lobe_totals.astype(jnp.bfloat16)
    mine_centers = lax.dynamic_slice_in_dim(centers, group_index * group_blocks, group_blocks, 0)
    lower_group = []
    upper_group = []
    for shift_by in range(1, ROUND_TOTAL + 1):
        partner = (group_index - shift_by) % group_count
        theirs = shifted(wave_patterns, "grp", shift_by)
        their_centers = lax.dynamic_slice_in_dim(centers, partner * group_blocks, group_blocks, 0)
        pair_flags = lax.dynamic_slice(
            near_flags,
            (group_index * group_blocks, partner * group_blocks),
            (group_blocks, group_blocks),
        )
        partial_sum = couple(
            wave_patterns,
            theirs,
            mine_centers,
            their_centers,
            pair_flags,
            heading,
            lobe_weights,
            near_boost,
        )
        coupled = lax.psum_scatter(
            partial_sum.astype(jnp.bfloat16), "sub", scatter_dimension=3, tiled=True
        ).astype(jnp.float32)
        lower_group.append(coupled)
        flipped = jnp.transpose(coupled, (1, 0, 3, 2))
        upper_group.append(
            shifted(flipped.astype(jnp.bfloat16), "grp", -shift_by).astype(flipped.dtype)
        )
    return (jnp.stack(lower_group, axis=1), jnp.stack(upper_group, axis=1))


def solution(mesh):
    placed = (
        P("grp", None, "sub"),
        P("grp", None, "sub"),
        P("grp", None, "sub"),
        P(),
        P(),
        P("sub"),
        P("sub"),
    )
    return jax.shard_map(
        shards,
        mesh=mesh,
        in_specs=placed,
        out_specs=(P("grp", None, None, None, "sub"), P("grp", None, None, "sub", None)),
        check_vma=False,
    )
```

profile of v0, /device:TPU:6, one launch (start us, length us, event | category | flops | bytes accessed | tf_op | source)
XLA Modules:
  0.0 488.2 jit_solution(5950489928034764180)
XLA Ops:
  7.2 0.0 copy-start
  7.2 0.0 all-gather.2.cloned.1.call-start
  7.2 0.7 all-gather.2.cloned.1.call-update
  7.9 0.0 all-reduce.5.cloned.1.call-start
  8.0 0.7 copy.14
  8.7 0.7 copy.15
  9.4 0.1 pad.8.clone
  9.5 57.0 %all_gather.9 = bf16[2,3,8192]{2,1,0:T(4,128)(2,1)S(1)} all-gather(bf16[2,3,512]{2,1,0:T(4,128)(2,1)S(1)} %copy.14), channel_id=1, replica_groups=mesh['grp'=32,'sub'=16] {'sub'}, dimensions={2}, use_global_device_ids=true | all-gather | bytes 104448 | tf_op jit(solution)/shard_map/all_gather | solution.py:82
  66.5 53.7 %all_gather.10 = bf16[2,3,8192]{2,1,0:T(4,128)(2,1)S(1)} all-gather(bf16[2,3,512]{2,1,0:T(4,128)(2,1)S(1)} %copy.15), channel_id=1, replica_groups=mesh['grp'=32,'sub'=16] {'sub'}, dimensions={2}, use_global_device_ids=true | all-gather | bytes 104448 | tf_op jit(solution)/shard_map/all_gather | solution.py:81
  120.2 0.1 fusion.58
  120.2 0.1 fusion.64
  120.3 0.1 fusion.66
  120.4 0.1 fusion.62
  120.5 0.0 copy-done
  120.5 0.3 fusion.44
  120.8 0.3 fusion.46
  121.0 0.3 fusion.48
  121.3 0.8 dynamic-slice_convert_fusion.1
  122.1 2.8 fusion.33
  124.9 33.0 %fusion.3 = (bf16[2,1,90,8192]{3,2,0,1:T(8,128)(2,1)S(1)}, bf16[2,1,90,8192]{3,2,0,1:T(8,128)(2,1)}) fusion(f32[90,2,8192]{2,0,1:T(8,128)S(1)} %fusion.33, bf16[2,3,8192]{2,1,0:T(4,128)(2,1)S(1)} %all_gather.10, f32[1,90]{1,0:T(1,128)S(1)} %get-tuple-element.26, f32[1,90]{1,0:T(1,128)S(1)} %get-tuple-element.30, f32[1,90]{1,0:T(1,128)S(1)} %get-tuple-element.32), kind=kOutput, calls=%fused_computation.7 | convolution fusion | flops 61932060 | bytes 11895864 | tf_op jit(solution)/shard_map/cl,bcu->blu/dot_general | solution.py:42
  157.9 79.5 %all-gather.2.cloned.1.call-done = bf16[2,240,8192]{2,1,0:T(8,128)(2,1)} async-done(((bf16[2,240,512]{2,1,0:T(8,128)(2,1)}), bf16[2,240,8192]{2,1,0:T(8,128)(2,1)}) %all-gather.2.cloned.1.call-update) | async-done | bytes 7864336 | tf_op jit(solution)/shard_map/all_gather | solution.py:80
  237.5 0.0 copy-start.1
  237.5 0.0 copy-start.2
  237.5 7.0 %fusion.9 = bf16[2,2,90,240]{3,2,1,0:T(8,128)(2,1)S(1)} fusion(bf16[2,240,8192]{2,1,0:T(8,128)(2,1)} %all-gather.2.cloned.1.call-done, bf16[2,1,90,8192]{3,2,0,1:T(8,128)(2,1)} %get-tuple-element.9, bf16[2,1,90,8192]{3,2,0,1:T(8,128)(2,1)S(1)} %get-tuple-element.8), kind=kOutput, calls=%fused_computation.15 | convolution fusion | flops 1418613120 | bytes 13935360 | tf_op jit(solution)/shard_map/bclu,bku->bclk/dot_general | solution.py:84
  244.4 1.9 collective-permute-start
  246.4 0.0 copy-done.1
  246.4 0.0 copy-done.2
  246.4 0.1 cosine_multiply_fusion.1
  246.5 4.0 collective-permute-start.1
  250.5 4.8 collective-permute-done
  255.4 0.5 fusion.14
  255.9 0.5 fusion.8
  256.3 1.2 copy.17
  257.5 1.2 collective-permute-done.1
  258.8 0.5 fusion.15
  259.3 0.5 fusion.7
  259.8 1.2 copy.18
  260.9 0.0 all-reduce.5.cloned.1.call-update
  261.0 1.3 dynamic-slice
  262.9 203.7 %all-reduce.5.cloned.1.call-done = (bf16[2,2,240,240]{2,1,0,3:T(2,128)(2,1)}, bf16[2,2,240,240]{2,1,0,3:T(2,128)(2,1)}) async-done(((bf16[2,2,240,240]{2,1,0,3:T(2,128)(2,1)}, bf16[2,2,240,240]{2,1,0,3:T(2,128)(2,1)}), (bf16[2,2,240,240]{2,1,0,3:T(2,128)(2,1)}, bf16[2,2,240,240]{2,1,0,3:T(2,128)(2,1)})) %all-reduce.5.cloned.1.call-update) | async-done | bytes 921616
  466.6 0.8 dynamic-slice_bitcast_fusion.2
  467.4 1.9 collective-permute-start.2
  469.3 0.8 dynamic-slice_bitcast_fusion
  470.1 8.9 %collective-permute-start.3 = (bf16[2,2,15,240]{3,0,1,2:T(2,128)(2,1)S(1)}, bf16[2,2,15,240]{3,0,1,2:T(2,128)(2,1)S(1)}, u32[]{:S(2)}, u32[]{:S(2)}) collective-permute-start(bf16[2,2,15,240]{3,0,1,2:T(2,128)(2,1)S(1)} %get-tuple-element.12), channel_id=1, source_target_pairs={{0,480},{16,496},{32,0},{48,16},{64,32},{80,48},{96,64},{112,80},{... | collective-permute-start | bytes 86408 | tf_op jit(solution)/shard_map/ppermute | solution.py:22
  479.0 0.1 maximum_convert_fusion
  479.1 0.7 copy.19
  479.8 0.0 collective-permute-done.2
  479.8 0.8 collective-permute-done.3
  480.6 0.1 maximum_convert_fusion.1
  480.7 0.7 copy.20
  (5 shorter events, 0.1 us)
Async XLA Ops:
  7.2 113.3 %copy-start = (f32[64,3]{0,1:T(4,128)S(1)}, f32[64,3]{0,1:T(4,128)}, u32[]{:S(2)}) copy-start(f32[64,3]{0,1:T(4,128)} %param.10) | copy-start | bytes 2308
  7.2 230.3 %all-gather.2.cloned.1.call-start = ((), (), s32[]{:S(2)}) async-start(), calls=%async_computation | async-start | bytes 8355840 | tf_op jit(solution)/shard_map/all_gather | solution.py:80
  7.9 458.7 %all-reduce.5.cloned.1.call-start = ((), (), s32[]{:S(2)}) async-start(), calls=%async_computation.1 | async-start | bytes 1966080
  237.5 8.9 %copy-start.1 = (f32[90]{0:T(128)S(1)}, f32[90]{0:T(128)}, u32[]{:S(2)}) copy-start(f32[90]{0:T(128)} %param.13) | copy-start | bytes 1084
  237.5 8.9 %copy-start.2 = (f32[90]{0:T(128)S(1)}, f32[90]{0:T(128)}, u32[]{:S(2)}) copy-start(f32[90]{0:T(128)} %param.12) | copy-start | bytes 1084
  244.4 10.9 %collective-permute-start = (bf16[2,2,90,240]{3,2,1,0:T(8,128)(2,1)S(1)}, bf16[2,2,90,240]{3,2,1,0:T(8,128)(2,1)S(1)}, u32[]{:S(2)}, u32[]{:S(2)}) collective-permute-start(bf16[2,2,90,240]{3,2,1,0:T(8,128)(2,1)S(1)} %fusion.9), channel_id=1, source_target_pairs={{0,16},{16,32},{32,48},{48,64},{64,80},{80,96},{96,112},{112,128},... | collective-permute-start | bytes 518408 | tf_op jit(solution)/shard_map/ppermute | solution.py:22
  246.5 12.3 %collective-permute-start.1 = (bf16[2,2,90,240]{3,2,1,0:T(8,128)(2,1)S(1)}, bf16[2,2,90,240]{3,2,1,0:T(8,128)(2,1)S(1)}, u32[]{:S(2)}, u32[]{:S(2)}) collective-permute-start(bf16[2,2,90,240]{3,2,1,0:T(8,128)(2,1)S(1)} %fusion.9), channel_id=1, source_target_pairs={{0,32},{16,48},{32,64},{48,80},{64,96},{80,112},{96,128},{112,144}... | collective-permute-start | bytes 518408 | tf_op jit(solution)/shard_map/ppermute | solution.py:22
  467.4 12.4 %collective-permute-start.2 = (bf16[2,2,15,240]{3,0,1,2:T(2,128)(2,1)S(1)}, bf16[2,2,15,240]{3,0,1,2:T(2,128)(2,1)S(1)}, u32[]{:S(2)}, u32[]{:S(2)}) collective-permute-start(bf16[2,2,15,240]{3,0,1,2:T(2,128)(2,1)S(1)} %get-tuple-element.10), channel_id=1, source_target_pairs={{0,496},{16,0},{32,16},{48,32},{64,48},{80,64},{96,80},{112,96},{1... | collective-permute-start | bytes 86408 | tf_op jit(solution)/shard_map/ppermute | solution.py:22
  470.1 10.5 %collective-permute-start.3 = (bf16[2,2,15,240]{3,0,1,2:T(2,128)(2,1)S(1)}, bf16[2,2,15,240]{3,0,1,2:T(2,128)(2,1)S(1)}, u32[]{:S(2)}, u32[]{:S(2)}) collective-permute-start(bf16[2,2,15,240]{3,0,1,2:T(2,128)(2,1)S(1)} %get-tuple-element.12), channel_id=1, source_target_pairs={{0,480},{16,496},{32,0},{48,16},{64,32},{80,48},{96,64},{112,80},{... | collective-permute-start | bytes 86408 | tf_op jit(solution)/shard_map/ppermute | solution.py:22
Sparse Core Ops, SparseCore 0:
  11.0 226.4 all-gather.1
  261.1 205.4 all-reduce.4
where the time goes:
time: 490 us; the launch traced here: 488 us
  waiting for transfers between devices  291 us (59%)
  blocking collectives  111 us (23%)
  matrix products  45.4 us (9%)
  starting transfers between devices  16.9 us (3%)
  between operations  14.9 us (3%)
  local copies, waits for them, and re-layouts  8.14 us (2%)
    unnamed x3, waiting for transfers between devices  204 us
    all_gather x1, waiting for transfers between devices, shards(): coeff_piece = lax.all_gather(coeffs, 'sub', axis=2, tiled=True)  79.5 us
    all_gather x1, blocking collectives, shards(): moment_piece = lax.all_gather(moments, 'sub', axis=2, tiled=True)  57 us
    all_gather x1, blocking collectives, shards(): offset_piece = lax.all_gather(offsets, 'sub', axis=2, tiled=True)  53.7 us
    dot_general x1, matrix products, samples(): jnp.einsum('cl,bcu->blu', heading, offsets.astype(jnp.float32), precision...  33 us
    ppermute x4, starting transfers between devices, shifted(): return lax.ppermute(value, axis, pairs)  16.8 us
  transfers between devices with their start and end apart: 6, of which 5 were waited for; matrix products, arithmetic and copies ran while one was open for 9% of the time, Pallas kernels for 0%

commit v1 on v0

v1 whole, which is shorter than its diff:
```python
import math

import jax
import jax.numpy as jnp
import numpy as np
from jax import lax
from jax.experimental import pallas as pl
from jax.experimental.pallas import tpu as pltpu
from jax.sharding import PartitionSpec as P

THETAS = 20
PHIS = 36
DIRS = 720
LOBE_TOTAL = 1440
ROUND_TOTAL = 2
BASIS = 240
RING = 4
HALF = 45
ROWS = 48
SLAB = 15
LANES = 256
DEPTH = 32
MESH = pl.DeviceIdType.MESH


def heading_of(t):
    theta = np.pi * ((t // PHIS) + 0.5) / THETAS
    azimuth = 2.0 * np.pi * (t % PHIS) / PHIS
    st, ct, sa, ca = np.sin(theta), np.cos(theta), np.sin(azimuth), np.cos(azimuth)
    heading = np.stack([st * ca, st * sa, ct], axis=-1)
    along_theta = np.stack([ct * ca, ct * sa, -st], axis=-1)
    along_phi = np.stack([-sa, ca, np.zeros_like(sa)], axis=-1)
    return heading, along_theta, along_phi


def split3(value):
    value = value.astype(np.float32)
    parts = []
    for _ in range(3):
        part = value.astype(jnp.bfloat16)
        parts.append(part)
        value = value - part.astype(np.float32)
    return np.concatenate(parts, axis=-1)


def grid_tables():
    pieces = np.zeros((RING, 3, 2, ROWS, DEPTH), jnp.bfloat16)
    headings = np.zeros((2 * RING, ROWS, 8), np.float32)
    places = np.full((2 * RING, ROWS, 8), -1, np.int32)
    for xo in range(RING):
        for dh in range(2):
            t = 90 * xo + HALF * dh + np.arange(HALF)
            heading, along_theta, along_phi = heading_of(t)
            pieces[xo, 0, dh, :HALF, 0:9] = split3(0.5 * heading)
            pieces[xo, 1, dh, :HALF, 9:18] = split3(along_theta)
            pieces[xo, 2, dh, :HALF, 9:18] = split3(along_phi)
            headings[2 * xo + dh, :HALF, 0:3] = 0.5 * heading
            opposite = PHIS * (THETAS - 1 - t // PHIS) + (t % PHIS + PHIS // 2) % PHIS
            places[2 * xo + dh, :HALF, 0] = t - 90 * xo
            places[2 * xo + dh, :HALF, 1] = opposite - 90 * (7 - xo)
            assert places[2 * xo + dh, :HALF].min(axis=0)[1] >= 0
            assert places[2 * xo + dh, :HALF].max(axis=0)[1] < 90
    return pieces.reshape(RING, 6 * ROWS, DEPTH), headings, places


def slab_matrix():
    matrix = np.zeros((LANES, LANES), jnp.bfloat16)
    for x in range(RING):
        for z in range(RING):
            for i in range(SLAB):
                matrix[(x * RING + z) * 16 + i, SLAB * (z * RING + x) + i] = 1
    return matrix


def turn_coefficients():
    nodes = np.cos(np.pi * (np.arange(400) + 0.5) / 400)
    square = 0.125 * (nodes + 1.0)
    r = np.sqrt(square)
    fit = np.polynomial.chebyshev.Chebyshev.fit
    cosine = fit(square, np.cos(2 * np.pi * r), 6, domain=[0, 0.25])
    sine = fit(square, -np.sin(2 * np.pi * r) / r, 5, domain=[0, 0.25])
    convert = np.polynomial.polynomial.Polynomial
    return (
        [float(v) for v in cosine.convert(kind=convert, domain=[-1, 1]).coef],
        [float(v) for v in sine.convert(kind=convert, domain=[-1, 1]).coef],
    )


COS_TERMS, SIN_TERMS = turn_coefficients()


def turn(s):
    r = s - jnp.round(s)
    y = r * r
    cosine = jnp.full_like(y, COS_TERMS[-1])
    for term in COS_TERMS[-2::-1]:
        cosine = cosine * y + term
    sine = jnp.full_like(y, SIN_TERMS[-1])
    for term in SIN_TERMS[-2::-1]:
        sine = sine * y + term
    return cosine, sine * r


def rounded(value):
    return value.astype(jnp.bfloat16)


def wide(value):
    return value.astype(jnp.float32)


class Copies:
    def __init__(self, send_sems, recv_sems):
        self.send_sems, self.recv_sems = send_sems, recv_sems
        self.all = []

    def start(self, source, target, device):
        place = len(self.all)
        copy = pltpu.make_async_remote_copy(
            src_ref=source,
            dst_ref=target,
            send_sem=self.send_sems.at[place],
            recv_sem=self.recv_sems.at[place],
            device_id=device,
            device_id_type=MESH,
        )
        copy.start()
        self.all.append(copy)
        return copy

    def finish(self):
        for copy in self.all:
            copy.wait_send()


class Ring:
    def __init__(self, copies, me, left, right, source, first, second, near, far):
        self.copies, self.left, self.right = copies, left, right
        self.across = source(lax.rem(me + 2, RING))
        self.after = source(lax.rem(me + 1, RING))
        self.before = source(lax.rem(me + 3, RING))
        self.own = source(me)
        self.first, self.second, self.near, self.far = first, second, near, far

    def step_1(self):
        self.from_left = self.copies.start(self.across.at[self.first], self.near.at[0], self.right)
        self.from_right = self.copies.start(self.across.at[self.second], self.near.at[1], self.left)

    def step_2(self):
        self.from_left.wait_recv()
        half = self.after.at[self.first]
        half[...] = rounded(wide(half[...]) + wide(self.near[0]))
        from_left = self.copies.start(self.after, self.far.at[0], self.right)
        self.from_right.wait_recv()
        half = self.before.at[self.second]
        half[...] = rounded(wide(half[...]) + wide(self.near[1]))
        from_right = self.copies.start(self.before, self.far.at[1], self.left)
        self.from_left, self.from_right = from_left, from_right

    def total(self):
        self.from_left.wait_recv()
        self.from_right.wait_recv()
        return wide(self.own[...]) + wide(self.far[0]) + wide(self.far[1])


N_COPIES = 3 + 2 * 2 * 4 + 4 + 2 * 2 * 4 + 2


def kernel(
    coeffs_ref, offsets_ref, moments_ref, centers_ref, flags_ref, weights_ref, boost_ref,
    pieces_ref, headings_ref, places_ref, slabs_ref,
    lower_ref, upper_ref,
    geometry, coeffs_pad, turned, samples, part, x_near, x_far, z_send, z_near, z_far,
    patterns, plain, theirs, lobe_send, lobe_recv,
    zp, zx_near, zx_far, zz_send, zz_near, zz_far, up_send, up_recv,
    send_sems, recv_sems,
):
    group = lax.axis_index("grp")
    groups = lax.axis_size("grp")
    sub = lax.axis_index("sub")
    x, z = lax.rem(sub, RING), sub // RING
    z_odd = lax.rem(z, 2)
    z_pair = z + 1 - 2 * z_odd

    def at(z_to, x_to):
        return {"sub": z_to * RING + x_to}

    x_right, x_left = at(z, lax.rem(x + 1, RING)), at(z, lax.rem(x + 3, RING))
    z_right, z_left = at(lax.rem(z + 1, RING), x), at(lax.rem(z + 3, RING), x)
    corner = at(z_pair, 3 - x)

    def other(shift):
        return {"grp": lax.rem(group + shift + groups, groups)}

    barrier = pltpu.get_barrier_semaphore()
    peers = [x_right, x_left, z_right, z_left, corner, other(1), other(-1), other(2), other(-2)]
    for peer in peers:
        pl.semaphore_signal(barrier, inc=1, device_id=peer, device_id_type=MESH)

    copies = Copies(send_sems, recv_sems)

    for block in range(2):
        geometry[block] = jnp.zeros((DEPTH, geometry.shape[2]), jnp.float32)
        for axis in range(3):
            offset = wide(offsets_ref[axis])[block : block + 1]
            moment = wide(moments_ref[axis])[block : block + 1]
            for piece in range(3):
                geometry[block, 3 * piece + axis : 3 * piece + axis + 1, :] = offset
                geometry[block, 9 + 3 * piece + axis : 10 + 3 * piece + axis, :] = moment
        coeffs_pad[block] = rounded(
            jnp.dot(slabs_ref[:, :BASIS], coeffs_ref[block], preferred_element_type=jnp.float32)
        )
    lobe_send[...] = jnp.zeros_like(lobe_send)
    lobe_send[0:1, 0 : weights_ref.shape[1]] = weights_ref[...]
    lobe_send[1:2, 0 : weights_ref.shape[1]] = boost_ref[...]

    def project(owner, block):
        turned[...] = jnp.dot(
            pieces_ref[owner], rounded(geometry[block]), preferred_element_type=jnp.float32
        )

        def rows_of(step, carried):
            low = pl.multiple_of(step * 16, 16)
            half, inner = step // 3, pl.multiple_of(lax.rem(step, 3) * 16, 16)
            cosine, sine = turn(turned[pl.ds(low, 16), :])
            for polar in range(2):
                weight = turned[pl.ds(low + (polar + 1) * 2 * ROWS, 16), :]
                samples[polar * 2 + half, 0, pl.ds(inner, 16), :] = rounded(weight * cosine)
                samples[polar * 2 + half, 1, pl.ds(inner, 16), :] = rounded(weight * sine)
            return carried

        lax.fori_loop(0, 6, rows_of, 0)
        sums = lax.dot_general(
            samples[...].reshape(8 * ROWS, samples.shape[3]),
            coeffs_pad[block],
            (((1,), (1,)), ((), ())),
            preferred_element_type=jnp.float32,
        )
        part[owner, block] = rounded(sums).reshape(4, 2, ROWS, LANES)

    across, after, before = lax.rem(x + 2, RING), lax.rem(x + 1, RING), lax.rem(x + 3, RING)
    x_rings = [
        Ring(
            copies, x, x_left, x_right, lambda o, b=b: part.at[o, b],
            pl.ds(0, 2), pl.ds(2, 2), x_near.at[b], x_far.at[b],
        )
        for b in range(2)
    ]
    z_rings = [
        Ring(
            copies, z, z_left, z_right, lambda o, b=b: z_send.at[b, o],
            0, 1, z_near.at[b], z_far.at[b],
        )
        for b in range(2)
    ]

    project(across, 0)
    pl.semaphore_wait(barrier, len(peers))
    x_rings[0].step_1()
    lobes = [
        copies.start(lobe_send, lobe_recv.at[k], peer)
        for k, peer in enumerate([at(z_pair, x), at(z, 3 - x), corner])
    ]
    project(across, 1)
    x_rings[1].step_1()
    project(after, 0)
    project(before, 0)
    x_rings[0].step_2()
    project(after, 1)
    project(before, 1)
    x_rings[1].step_2()
    project(x, 0)
    z_send[0] = rounded(x_rings[0].total())
    z_rings[0].step_1()
    project(x, 1)
    z_rings[0].step_2()
    z_send[1] = rounded(x_rings[1].total())
    z_rings[1].step_1()

    to_groups = []

    def settle(block):
        patterns[block] = rounded(z_rings[block].total())
        for r in range(ROUND_TOTAL):
            to_groups.append(copies.start(patterns.at[block], theirs.at[r, block], other(r + 1)))
        plain[block] = rounded(
            jnp.dot(
                patterns[block].reshape(2 * ROWS, LANES), slabs_ref[...], preferred_element_type=jnp.float32
            )
        )

    settle(0)
    z_rings[1].step_2()

    for lobe in lobes:
        lobe.wait_recv()
    odd = z_odd.astype(jnp.float32)
    lane = lax.broadcasted_iota(jnp.int32, (ROWS, 128), 1)
    place = places_ref[x * 2 + z_odd]
    heading = headings_ref[x * 2 + z_odd]

    def lobe_column(row):
        near = lobe_send[row : row + 1, :] * (1.0 - odd) + lobe_recv[0, row : row + 1, :] * odd
        far = lobe_recv[2, row : row + 1, :] * (1.0 - odd) + lobe_recv[1, row : row + 1, :] * odd
        picked = jnp.where(lane == place[:, 0:1], near, 0.0) + jnp.where(lane == place[:, 1:2], far, 0.0)
        return jnp.sum(picked, axis=1, keepdims=True)

    weight_sum, boost_sum = lobe_column(0), lobe_column(1)
    pair_lane = lax.broadcasted_iota(jnp.int32, (1, 128), 1)
    flag_row = jnp.zeros((1, 128), jnp.float32)
    offset_rows = [jnp.zeros((1, 128), jnp.float32) for _ in range(3)]
    for r in range(ROUND_TOTAL):
        partner = lax.rem(group - r - 1 + groups, groups)
        for i in range(2):
            for j in range(2):
                m, n = group * 2 + i, partner * 2 + j
                here = pair_lane == (r * 4 + i * 2 + j)
                flag_row = jnp.where(here, flags_ref[m, n].astype(jnp.float32), flag_row)
                for axis in range(3):
                    gap = centers_ref[axis, m] - centers_ref[axis, n]
                    offset_rows[axis] = jnp.where(here, gap, offset_rows[axis])
    cosine, sine = turn(
        heading[:, 0:1] * offset_rows[0] + heading[:, 1:2] * offset_rows[1] + heading[:, 2:3] * offset_rows[2]
    )
    amplitude = (weight_sum + flag_row * boost_sum) * (1.0 / math.sqrt(LOBE_TOTAL))
    cosine, sine = amplitude * cosine, amplitude * sine

    zx_rings = [
        Ring(
            copies, x, x_left, x_right, lambda o, r=r: zp.at[o, r],
            pl.ds(0, 2), pl.ds(2, 2), zx_near.at[r], zx_far.at[r],
        )
        for r in range(ROUND_TOTAL)
    ]
    zz_rings = [
        Ring(
            copies, z, z_left, z_right, lambda o, r=r: zz_send.at[r, o],
            pl.ds(0, 2), pl.ds(2, 2), zz_near.at[r], zz_far.at[r],
        )
        for r in range(ROUND_TOTAL)
    ]
    settle(1)

    for r in range(ROUND_TOTAL):
        for j in range(2):
            to_groups[2 * j + r].wait_recv()
            real, imag = wide(theirs[r, j, 0]), wide(theirs[r, j, 1])
            for i in range(2):
                pair = i * 2 + j
                lane_at = r * 4 + pair
                c, s = cosine[:, lane_at : lane_at + 1], sine[:, lane_at : lane_at + 1]
                carry = jnp.concatenate([rounded(c * real + s * imag), rounded(c * imag - s * real)], axis=0)
                z_part = rounded(
                    lax.dot_general(
                        carry, plain[i], (((0,), (0,)), ((), ())), preferred_element_type=jnp.float32
                    )
                )
                for to_x in range(RING):
                    for to_z in range(RING):
                        low = (to_x * RING + to_z) * 16
                        zp[to_x, r, to_z, pair] = z_part[low : low + 16]
        zx_rings[r].step_1()

    zx_rings[0].step_2()
    zx_rings[1].step_2()
    zz_send[0] = rounded(zx_rings[0].total())
    zz_rings[0].step_1()
    zz_send[1] = rounded(zx_rings[1].total())
    zz_rings[1].step_1()
    zz_rings[0].step_2()
    zz_rings[1].step_2()

    back = []
    for r in range(ROUND_TOTAL):
        total = zz_rings[r].total()
        up_send[r] = rounded(total)
        back.append(copies.start(up_send.at[r], up_recv.at[r], other(-r - 1)))
        for i in range(2):
            for j in range(2):
                lower_ref[i, r, :, j, :] = total[i * 2 + j, :SLAB, :BASIS]
    for r in range(ROUND_TOTAL):
        back[r].wait_recv()
        for i in range(2):
            for j in range(2):
                upper_ref[j, r, :, i, :] = wide(up_recv[r, i * 2 + j])[:SLAB, :BASIS]
    copies.finish()


def shards(coeffs, offsets, moments, centers, near_flags, lobe_weights, near_boost):
    pieces, headings, places = grid_tables()
    unknowns = coeffs.shape[2]
    bf16, f32 = jnp.bfloat16, jnp.float32
    vmem = pl.BlockSpec(memory_space=pltpu.VMEM)
    smem = pl.BlockSpec(memory_space=pltpu.SMEM)
    out = jax.ShapeDtypeStruct((2, ROUND_TOTAL, SLAB, 2, BASIS), f32)
    lower, upper = pl.pallas_call(
        kernel,
        out_shape=(out, out),
        in_specs=[vmem, vmem, vmem, smem, smem, vmem, vmem, vmem, vmem, vmem, vmem],
        out_specs=(vmem, vmem),
        scratch_shapes=[
            pltpu.VMEM((2, DEPTH, unknowns), f32),
            pltpu.VMEM((2, LANES, unknowns), bf16),
            pltpu.VMEM((6 * ROWS, unknowns), f32),
            pltpu.VMEM((4, 2, ROWS, unknowns), bf16),
            pltpu.VMEM((RING, 2, RING, 2, ROWS, LANES), bf16),
            pltpu.VMEM((2, 2, 2, 2, ROWS, LANES), bf16),
            pltpu.VMEM((2, 2, RING, 2, ROWS, LANES), bf16),
            pltpu.VMEM((2, RING, 2, ROWS, LANES), bf16),
            pltpu.VMEM((2, 2, ROWS, LANES), bf16),
            pltpu.VMEM((2, 2, 2, ROWS, LANES), bf16),
            pltpu.VMEM((2, 2, ROWS, LANES), bf16),
            pltpu.VMEM((2, 2 * ROWS, LANES), bf16),
            pltpu.VMEM((ROUND_TOTAL, 2, 2, ROWS, LANES), bf16),
            pltpu.VMEM((8, 128), f32),
            pltpu.VMEM((3, 8, 128), f32),
            pltpu.VMEM((RING, ROUND_TOTAL, RING, 4, 16, LANES), bf16),
            pltpu.VMEM((ROUND_TOTAL, 2, 2, 4, 16, LANES), bf16),
            pltpu.VMEM((ROUND_TOTAL, 2, RING, 4, 16, LANES), bf16),
            pltpu.VMEM((ROUND_TOTAL, RING, 4, 16, LANES), bf16),
            pltpu.VMEM((ROUND_TOTAL, 2, 2, 16, LANES), bf16),
            pltpu.VMEM((ROUND_TOTAL, 2, 4, 16, LANES), bf16),
            pltpu.VMEM((ROUND_TOTAL, 4, 16, LANES), bf16),
            pltpu.VMEM((ROUND_TOTAL, 4, 16, LANES), bf16),
            pltpu.SemaphoreType.DMA((N_COPIES,)),
            pltpu.SemaphoreType.DMA((N_COPIES,)),
        ],
        compiler_params=pltpu.CompilerParams(
            collective_id=0, has_side_effects=True, vmem_limit_bytes=40 * 1024 * 1024
        ),
        name="fill",
    )(
        coeffs,
        jnp.transpose(offsets, (1, 0, 2)),
        jnp.transpose(moments, (1, 0, 2)),
        jnp.transpose(centers),
        near_flags,
        lobe_weights.reshape(1, -1),
        near_boost.reshape(1, -1),
        jnp.asarray(pieces),
        jnp.asarray(headings),
        jnp.asarray(places),
        jnp.asarray(slab_matrix()),
    )
    return jnp.transpose(lower, (0, 1, 3, 4, 2)), jnp.transpose(upper, (0, 1, 3, 2, 4))


def solution(mesh):
    placed = (
        P("grp", None, "sub"),
        P("grp", None, "sub"),
        P("grp", None, "sub"),
        P(),
        P(),
        P("sub"),
        P("sub"),
    )
    return jax.shard_map(
        shards,
        mesh=mesh,
        in_specs=placed,
        out_specs=(P("grp", None, None, None, "sub"), P("grp", None, None, "sub", None)),
        check_vma=False,
    )
```

time: 490 us -> 87.5 us (0.18)
  the two profiles are of different devices: /device:TPU:6 before, /device:TPU:16 now
where the time goes in v1:
time: 87.5 us; the launch traced here: 87.1 us
  Pallas kernels  78.2 us (89%)
  local copies, waits for them, and re-layouts  8.17 us (9%)
    pallas_call x1, Pallas kernels, shards(): pl.pallas_call(kernel, out_shape=(out, out), in_specs=[vmem, vmem, vmem,...  78.2 us
    unnamed x24, local copies, waits for them, and re-layouts  8.17 us

profile of v1, /device:TPU:16, one launch (start us, length us, event | category | flops | bytes accessed | tf_op | source)
XLA Modules:
  0.0 87.1 jit_solution(17356927969477309904)
XLA Ops:
  0.6 0.0 copy-start.6
  0.6 0.0 copy-start.8
  0.7 0.0 copy-start.9
  0.7 0.0 copy-start.10
  0.7 0.7 copy-done.6
  1.3 0.0 copy-done.8
  1.3 0.0 copy-done.9
  1.3 0.0 copy-done.10
  1.3 0.0 copy-start
  1.3 1.0 %copy-done = bf16[2,240,512]{2,1,0:T(8,128)(2,1)S(1)} copy-done((bf16[2,240,512]{2,1,0:T(8,128)(2,1)S(1)}, bf16[2,240,512]{2,1,0:T(8,128)(2,1)}, u32[]{:S(2)}) %copy-start) | copy-done | bytes 491544
  2.4 0.0 copy-start.1
  2.4 1.0 %copy-done.1 = bf16[4,288,32]{2,1,0:T(8,128)(2,1)S(1)} copy-done((bf16[4,288,32]{2,1,0:T(8,128)(2,1)S(1)}, bf16[4,288,32]{2,1,0:T(8,128)(2,1)}, u32[]{:S(2)}) %copy-start.1) | copy-done | bytes 73752
  3.3 0.0 copy-start.2
  3.3 0.9 %copy-done.2 = s32[8,48,8]{2,1,0:T(8,128)S(1)} copy-done((s32[8,48,8]{2,1,0:T(8,128)S(1)}, s32[8,48,8]{2,1,0:T(8,128)}, u32[]{:S(2)}) %copy-start.2) | copy-done | bytes 12312
  4.3 0.0 copy-start.3
  4.3 0.9 %copy-done.3 = f32[8,48,8]{2,1,0:T(8,128)S(1)} copy-done((f32[8,48,8]{2,1,0:T(8,128)S(1)}, f32[8,48,8]{2,1,0:T(8,128)}, u32[]{:S(2)}) %copy-start.3) | copy-done | bytes 12312
  5.2 0.0 copy-start.4
  5.2 0.9 %copy-done.4 = bf16[256,256]{1,0:T(8,128)(2,1)S(1)} copy-done((bf16[256,256]{1,0:T(8,128)(2,1)S(1)}, bf16[256,256]{1,0:T(8,128)(2,1)}, u32[]{:S(2)}) %copy-start.4) | copy-done | bytes 131096
  6.1 0.0 copy-start.5
  6.1 0.8 copy-done.5
  6.8 0.0 copy-start.7
  6.8 0.7 copy-done.7
  7.5 78.2 %fill.1 = (f32[2,2,15,2,240]{4,3,2,1,0:T(2,128)S(1)}, f32[2,2,15,2,240]{4,3,2,1,0:T(2,128)S(1)}) custom-call(bf16[2,240,512]{2,1,0:T(8,128)(2,1)S(1)} %copy-done, bf16[3,2,512]{2,1,0:T(2,128)(2,1)S(1)} %bitcast.9, bf16[3,2,512]{2,1,0:T(2,128)(2,1)S(1)} %bitcast.10, f32[3,64]{1,0:T(4,128)S(1)} %bitcast.11, s32[64,64]{1,0:T(8,128)S(1)} %copy-done.5, ...), custom_call_target="tpu_custom_call" | custom-call | tf_op jit(solution)/shard_map/fill/pallas_call | solution.py:396
  85.8 0.7 copy.15
  86.4 0.6 copy.16
Async XLA Ops:
  0.6 0.7 copy-start.6
  0.6 0.7 copy-start.8
  0.7 0.7 copy-start.9
  0.7 0.7 copy-start.10
  1.3 1.0 %copy-start = (bf16[2,240,512]{2,1,0:T(8,128)(2,1)S(1)}, bf16[2,240,512]{2,1,0:T(8,128)(2,1)}, u32[]{:S(2)}) copy-start(bf16[2,240,512]{2,1,0:T(8,128)(2,1)} %coeffs_ref.1) | copy-start | bytes 1474564
  2.4 1.0 %copy-start.1 = (bf16[4,288,32]{2,1,0:T(8,128)(2,1)S(1)}, bf16[4,288,32]{2,1,0:T(8,128)(2,1)}, u32[]{:S(2)}) copy-start(bf16[4,288,32]{2,1,0:T(8,128)(2,1)} %constant.8.clone.pieces_ref) | copy-start | bytes 221188
  3.3 0.9 %copy-start.2 = (s32[8,48,8]{2,1,0:T(8,128)S(1)}, s32[8,48,8]{2,1,0:T(8,128)}, u32[]{:S(2)}) copy-start(s32[8,48,8]{2,1,0:T(8,128)} %constant.10.clone.places_ref) | copy-start | bytes 36868
  4.3 0.9 %copy-start.3 = (f32[8,48,8]{2,1,0:T(8,128)S(1)}, f32[8,48,8]{2,1,0:T(8,128)}, u32[]{:S(2)}) copy-start(f32[8,48,8]{2,1,0:T(8,128)} %constant.9.clone.headings_ref) | copy-start | bytes 36868
  5.2 0.9 %copy-start.4 = (bf16[256,256]{1,0:T(8,128)(2,1)S(1)}, bf16[256,256]{1,0:T(8,128)(2,1)}, u32[]{:S(2)}) copy-start(bf16[256,256]{1,0:T(8,128)(2,1)} %constant.11.clone.slabs_ref) | copy-start | bytes 393220
  6.1 0.8 copy-start.5
  6.8 0.7 copy-start.7

commit v2 on v1

v2 whole, which is shorter than its diff:
```python
import math

import jax
import jax.numpy as jnp
import numpy as np
from jax import lax
from jax.experimental import pallas as pl
from jax.experimental.pallas import tpu as pltpu
from jax.sharding import PartitionSpec as P

THETAS = 20
PHIS = 36
DIRS = 720
LOBE_TOTAL = 1440
ROUND_TOTAL = 2
BASIS = 240
RING = 4
HALF = 45
ROWS = 48
HOLD = 64
SLAB = 15
LANES = 256
DEPTH = 32
MESH = pl.DeviceIdType.MESH


def heading_of(t):
    theta = np.pi * ((t // PHIS) + 0.5) / THETAS
    azimuth = 2.0 * np.pi * (t % PHIS) / PHIS
    st, ct, sa, ca = np.sin(theta), np.cos(theta), np.sin(azimuth), np.cos(azimuth)
    heading = np.stack([st * ca, st * sa, ct], axis=-1)
    along_theta = np.stack([ct * ca, ct * sa, -st], axis=-1)
    along_phi = np.stack([-sa, ca, np.zeros_like(sa)], axis=-1)
    return heading, along_theta, along_phi


def split3(value):
    value = value.astype(np.float32)
    parts = []
    for _ in range(3):
        part = value.astype(jnp.bfloat16)
        parts.append(part)
        value = value - part.astype(np.float32)
    return np.concatenate(parts, axis=-1)


def grid_tables():
    pieces = np.zeros((RING, 3, 2, ROWS, DEPTH), jnp.bfloat16)
    headings = np.zeros((2 * RING, 8, 2, HOLD), np.float32)
    places = np.full((2 * RING, 8, 2, HOLD), -1, np.int32)
    for xo in range(RING):
        for dh in range(2):
            t = 90 * xo + HALF * dh + np.arange(HALF)
            heading, along_theta, along_phi = heading_of(t)
            pieces[xo, 0, dh, :HALF, 0:9] = split3(0.5 * heading)
            pieces[xo, 1, dh, :HALF, 9:18] = split3(along_theta)
            pieces[xo, 2, dh, :HALF, 9:18] = split3(along_phi)
            headings[2 * xo + dh, 0:3, :, :HALF] = 0.5 * heading.T[:, None]
            opposite = PHIS * (THETAS - 1 - t // PHIS) + (t % PHIS + PHIS // 2) % PHIS - 90 * (7 - xo)
            assert opposite.min() >= 0 and opposite.max() < 90
            places[2 * xo + dh, 0, :, :HALF] = t - 90 * xo
            places[2 * xo + dh, 1, :, :HALF] = opposite
    wide_as = (2 * RING, 8, 2 * HOLD)
    return pieces.reshape(RING, 6 * ROWS, DEPTH), headings.reshape(wide_as), places.reshape(wide_as)


def turn_coefficients():
    nodes = np.cos(np.pi * (np.arange(400) + 0.5) / 400)
    square = 0.125 * (nodes + 1.0)
    r = np.sqrt(square)
    fit = np.polynomial.chebyshev.Chebyshev.fit
    cosine = fit(square, np.cos(2 * np.pi * r), 6, domain=[0, 0.25])
    sine = fit(square, -np.sin(2 * np.pi * r) / r, 5, domain=[0, 0.25])
    convert = np.polynomial.polynomial.Polynomial
    return (
        [float(v) for v in cosine.convert(kind=convert, domain=[-1, 1]).coef],
        [float(v) for v in sine.convert(kind=convert, domain=[-1, 1]).coef],
    )


COS_TERMS, SIN_TERMS = turn_coefficients()


def turn(s):
    r = s - jnp.round(s)
    y = r * r
    cosine = jnp.full_like(y, COS_TERMS[-1])
    for term in COS_TERMS[-2::-1]:
        cosine = cosine * y + term
    sine = jnp.full_like(y, SIN_TERMS[-1])
    for term in SIN_TERMS[-2::-1]:
        sine = sine * y + term
    return cosine, sine * r


def rounded(value):
    return value.astype(jnp.bfloat16)


def wide(value):
    return value.astype(jnp.float32)


class Copies:
    def __init__(self, send_sems, recv_sems):
        self.send_sems, self.recv_sems = send_sems, recv_sems
        self.all = []

    def start(self, source, target, device):
        place = len(self.all)
        copy = pltpu.make_async_remote_copy(
            src_ref=source,
            dst_ref=target,
            send_sem=self.send_sems.at[place],
            recv_sem=self.recv_sems.at[place],
            device_id=device,
            device_id_type=MESH,
        )
        copy.start()
        self.all.append(copy)
        return copy

    def finish(self):
        for copy in self.all:
            copy.wait_send()


class Ring:
    def __init__(self, copies, me, left, right, source, first, second, near, far):
        self.copies, self.left, self.right = copies, left, right
        self.across = source(lax.rem(me + 2, RING))
        self.after = source(lax.rem(me + 1, RING))
        self.before = source(lax.rem(me + 3, RING))
        self.own = source(me)
        self.first, self.second, self.near, self.far = first, second, near, far

    def step_1(self):
        self.from_left = self.copies.start(self.across.at[self.first], self.near.at[0], self.right)
        self.from_right = self.copies.start(self.across.at[self.second], self.near.at[1], self.left)

    def step_2(self):
        self.from_left.wait_recv()
        half = self.after.at[self.first]
        half[...] = rounded(wide(half[...]) + wide(self.near[0]))
        from_left = self.copies.start(self.after, self.far.at[0], self.right)
        self.from_right.wait_recv()
        half = self.before.at[self.second]
        half[...] = rounded(wide(half[...]) + wide(self.near[1]))
        from_right = self.copies.start(self.before, self.far.at[1], self.left)
        self.from_left, self.from_right = from_left, from_right

    def total(self):
        self.from_left.wait_recv()
        self.from_right.wait_recv()
        return wide(self.own[...]) + wide(self.far[0]) + wide(self.far[1])


PAIRS = [(0, 0, 0), (1, 0, 0), (0, 0, 1), (0, 1, 0), (0, 1, 1), (1, 0, 1), (1, 1, 0), (1, 1, 1)]
PARTS = [(0, 2), (2, 5), (5, 8)]
UPWARD = [[(0, 1), (1, 2)], [(2, 5)], [(5, 8)]]
N_COPIES = 4 + 4 * 4 + 4 * 4 + 2 * 3 + 2 * 8 + 3 * 3 + 4


def slab_matrix():
    place = lax.broadcasted_iota(jnp.int32, (LANES, LANES), 0)
    function = lax.broadcasted_iota(jnp.int32, (LANES, LANES), 1)
    x, z, i = place // 64, (place // 16) % RING, place % 16
    held = jnp.where(i < SLAB, SLAB * (z * RING + x) + i, -1)
    return jnp.where(held == function, 1.0, 0.0).astype(jnp.bfloat16)


def kernel(
    coeffs_hbm, offsets_hbm, moments_hbm, centers_hbm, flags_hbm, weights_hbm, boost_hbm,
    pieces_hbm, headings_hbm, places_hbm,
    lower_ref, upper_ref,
    coeffs_ref, offsets_ref, moments_ref, centers_ref, flags_ref, weights_ref, boost_ref,
    pieces_ref, headings_ref, places_ref,
    slabs, geometry, coeffs_pad, turned, samples, part, x_near, x_far, z_send, z_near, z_far,
    patterns, plain, turned_send, turned_recv, lobe_pair, lobe_all,
    zp, z_recv, up_send, up_recv,
    send_sems, recv_sems, load_sems,
):
    group = lax.axis_index("grp")
    groups = lax.axis_size("grp")
    sub = lax.axis_index("sub")
    x, z = lax.rem(sub, RING), sub // RING
    z_odd = lax.rem(z, 2)

    def at(z_to, x_to):
        return {"sub": z_to * RING + x_to}

    def along(me, steps):
        return lax.rem(me + steps, RING)

    x_peers = [at(z, along(x, d)) for d in range(1, RING)]
    z_peers = [at(along(z, d), x) for d in range(1, RING)]
    z_pair = at(z + 1 - 2 * z_odd, x)

    def other(shift, d=0):
        return {"grp": lax.rem(group + shift + groups, groups), "sub": z * RING + along(x, d)}

    plain[:, :, :, ROWS:] = jnp.zeros((2, RING, 2, HOLD - ROWS, LANES), jnp.bfloat16)

    barrier = pltpu.get_barrier_semaphore()
    group_peers = [other(shift, d) for shift in (1, -1, 2, -2) for d in range(RING)]
    peers = x_peers + z_peers + group_peers
    for peer in peers:
        pl.semaphore_signal(barrier, inc=1, device_id=peer, device_id_type=MESH)

    loads = [
        pltpu.make_async_copy(source, target, load_sems.at[k])
        for k, (source, target) in enumerate(
            [
                (offsets_hbm, offsets_ref),
                (moments_hbm, moments_ref),
                (pieces_hbm, pieces_ref),
                (coeffs_hbm, coeffs_ref),
                (weights_hbm, weights_ref),
                (boost_hbm, boost_ref),
                (centers_hbm, centers_ref),
                (flags_hbm, flags_ref),
                (headings_hbm, headings_ref),
                (places_hbm, places_ref),
            ]
        )
    ]
    for load in loads:
        load.start()

    copies = Copies(send_sems, recv_sems)
    slabs[...] = slab_matrix()
    for load in loads[:4]:
        load.wait()

    for block in range(2):
        geometry[block] = jnp.zeros((DEPTH, geometry.shape[2]), jnp.float32)
        for axis in range(3):
            offset = wide(offsets_ref[axis])[block : block + 1]
            moment = wide(moments_ref[axis])[block : block + 1]
            for piece in range(3):
                geometry[block, 3 * piece + axis : 3 * piece + axis + 1, :] = offset
                geometry[block, 9 + 3 * piece + axis : 10 + 3 * piece + axis, :] = moment
        coeffs_pad[block] = rounded(
            jnp.dot(slabs[:, :BASIS], coeffs_ref[block], preferred_element_type=jnp.float32)
        )

    def project(owner, block):
        turned[...] = jnp.dot(
            pieces_ref[owner], rounded(geometry[block]), preferred_element_type=jnp.float32
        )

        def rows_of(step, carried):
            low = pl.multiple_of(step * 16, 16)
            half, inner = step // 3, pl.multiple_of(lax.rem(step, 3) * 16, 16)
            cosine, sine = turn(turned[pl.ds(low, 16), :])
            for polar in range(2):
                weight = turned[pl.ds(low + (polar + 1) * 2 * ROWS, 16), :]
                samples[0, polar * 2 + half, pl.ds(inner, 16), :] = rounded(weight * cosine)
                samples[1, polar * 2 + half, pl.ds(inner, 16), :] = rounded(weight * sine)
            return carried

        lax.fori_loop(0, 6, rows_of, 0)
        sums = lax.dot_general(
            samples[...].reshape(8 * ROWS, samples.shape[3]),
            coeffs_pad[block],
            (((1,), (1,)), ((), ())),
            preferred_element_type=jnp.float32,
        )
        for side in range(2):
            part[owner, block, :, :, side] = rounded(sums[:, side * 128 : side * 128 + 128]).reshape(
                2, RING, ROWS, 128
            )

    across, after, before = along(x, 2), along(x, 1), along(x, 3)
    steps = [(b, c) for b in range(2) for c in range(2)]
    x_rings = [
        Ring(
            copies, x, x_peers[2], x_peers[0], lambda o, b=b, c=c: part.at[o, b, c],
            pl.ds(0, 2), pl.ds(2, 2), x_near.at[k], x_far.at[k],
        )
        for k, (b, c) in enumerate(steps)
    ]
    z_rings = [
        Ring(
            copies, z, z_peers[2], z_peers[0], lambda o, k=k: z_send.at[k, o],
            0, 1, z_near.at[k], z_far.at[k],
        )
        for k in range(4)
    ]

    def cross(k):
        z_send[k] = rounded(x_rings[k].total())
        z_rings[k].step_1()

    def keep(k):
        total = z_rings[k].total()
        for side in range(2):
            patterns[k // 2, k % 2, 0:ROWS, side * 128 : side * 128 + 128] = total[side]

    project(across, 0)
    pl.semaphore_wait(barrier, len(peers))
    x_rings[0].step_1()
    x_rings[1].step_1()
    project(across, 1)
    x_rings[2].step_1()
    x_rings[3].step_1()

    loads[4].wait()
    loads[5].wait()
    lobe_pair[0] = jnp.zeros((8, 128), jnp.float32)
    lobe_pair[0, 0:1, 0 : weights_ref.shape[1]] = weights_ref[...]
    lobe_pair[0, 1:2, 0 : weights_ref.shape[1]] = boost_ref[...]
    paired = copies.start(lobe_pair.at[0], lobe_pair.at[1], z_pair)

    project(after, 0)
    project(before, 0)
    x_rings[0].step_2()
    x_rings[1].step_2()
    project(after, 1)
    project(before, 1)
    x_rings[2].step_2()
    x_rings[3].step_2()
    project(x, 0)
    project(x, 1)
    paired.wait_recv()
    lobe_all[0] = lobe_pair[...]
    lobes = [copies.start(lobe_all.at[0], lobe_all.at[d], x_peers[d - 1]) for d in range(1, RING)]
    patterns[...] = jnp.zeros_like(patterns)
    cross(0)
    cross(1)
    z_rings[0].step_2()
    cross(2)
    z_rings[1].step_2()
    cross(3)
    z_rings[2].step_2()

    gathered = {}

    def settle(block):
        pattern = rounded(patterns[block])
        turned_send[block] = rounded(jnp.transpose(wide(pattern).reshape(2 * HOLD, LANES))).reshape(
            RING, HOLD, 2 * HOLD
        )
        for r in range(ROUND_TOTAL):
            for d in range(RING):
                gathered[block, r, d] = copies.start(
                    turned_send.at[block, along(x, d)], turned_recv.at[r, block, d], other(r + 1, d)
                )
        rows = pl.ds(0, ROWS)
        plain[block, 0, :, rows] = rounded(
            jnp.dot(pattern.reshape(2 * HOLD, LANES), slabs[...], preferred_element_type=jnp.float32)
        ).reshape(2, HOLD, LANES)[:, :ROWS]
        for d in range(1, RING):
            gathered[block, d] = copies.start(
                plain.at[block, 0, :, rows], plain.at[block, d, :, rows], x_peers[d - 1]
            )

    keep(0)
    keep(1)
    settle(0)
    z_rings[3].step_2()

    for load in loads[6:]:
        load.wait()
    row = lax.broadcasted_iota(jnp.int32, (8, 128), 0)
    flag_column = jnp.zeros((8, 128), jnp.float32)
    gaps = [jnp.zeros((8, 128), jnp.float32) for _ in range(3)]
    for k, (r, i, j) in enumerate(PAIRS):
        m = group * 2 + i
        n = lax.rem(group - r - 1 + groups, groups) * 2 + j
        flag_column = jnp.where(row == k, flags_ref[m, n].astype(jnp.float32), flag_column)
        for axis in range(3):
            gap = centers_ref[axis, m] - centers_ref[axis, n]
            gaps[axis] = jnp.where(row == k, gap, gaps[axis])
    odd = z_odd.astype(jnp.float32)
    below = lax.broadcasted_iota(jnp.int32, (128, 128), 0)
    sign = jnp.where(lax.broadcasted_iota(jnp.int32, (8, 128), 1) < HOLD, 1.0, -1.0)
    for lobe in lobes:
        lobe.wait_recv()
    cosines, sines = [], []
    for d in range(RING):
        source = lax.rem(x - d + RING, RING)
        facing = lax.rem(2 * x - d - 3 + 2 * RING, RING)
        table = source * 2 + z_odd
        near = lobe_all[d, 0] * (1.0 - odd) + lobe_all[d, 1] * odd
        far = lobe_all[facing, 1] * (1.0 - odd) + lobe_all[facing, 0] * odd
        place = places_ref[table]
        sums = jnp.dot(
            near, jnp.where(below == place[0:1], 1.0, 0.0),
            precision=lax.Precision.HIGHEST, preferred_element_type=jnp.float32,
        ) + jnp.dot(
            far, jnp.where(below == place[1:2], 1.0, 0.0),
            precision=lax.Precision.HIGHEST, preferred_element_type=jnp.float32,
        )
        heading = headings_ref[table]
        cosine, sine = turn(heading[0:1] * gaps[0] + heading[1:2] * gaps[1] + heading[2:3] * gaps[2])
        amplitude = (sums[0:1] + flag_column * sums[1:2]) * (1.0 / math.sqrt(LOBE_TOTAL))
        cosines.append(amplitude * cosine)
        sines.append(amplitude * sine * sign)

    def couple(k):
        r, i, j = PAIRS[k]
        carries = []
        for d in range(RING):
            right = wide(turned_recv[r, j, d])
            carries.append(
                rounded(
                    cosines[d][k : k + 1] * right + sines[d][k : k + 1] * pltpu.roll(right, HOLD, 1)
                )
            )
        total = jnp.dot(
            jnp.concatenate(carries, axis=1),
            plain[i].reshape(RING * 2 * HOLD, LANES),
            preferred_element_type=jnp.float32,
        )
        zp[:, k] = rounded(total).reshape(RING, 16, LANES)

    def arrived(block, rounds):
        for r in rounds:
            for d in range(RING):
                gathered[block, r, d].wait_recv()

    def arrived_own(block):
        for d in range(1, RING):
            gathered[block, d].wait_recv()

    spread = []

    def scatter(p):
        low, high = PARTS[p]
        for k in range(low, high):
            couple(k)
        pairs = pl.ds(low, high - low)
        spread.append(
            [
                copies.start(zp.at[along(z, d), pairs], z_recv.at[d - 1, pairs], z_peers[d - 1])
                for d in range(1, RING)
            ]
        )

    arrived(0, [0, 1])
    arrived_own(0)
    scatter(0)
    keep(2)
    keep(3)
    settle(1)
    arrived(1, [0])
    arrived_own(1)
    scatter(1)
    arrived(1, [1])
    scatter(2)

    back = []
    for p, (low, high) in enumerate(PARTS):
        for copy in spread[p]:
            copy.wait_recv()
        pairs = pl.ds(low, high - low)
        total = wide(zp[z, pairs])
        for d in range(1, RING):
            total = total + wide(z_recv[d - 1, pairs])
        up_send[pairs] = rounded(total)
        for first, last in UPWARD[p]:
            mine = pl.ds(first, last - first)
            back.append(copies.start(up_send.at[mine], up_recv.at[mine], other(-PAIRS[first][0] - 1)))
        for k in range(low, high):
            r, i, j = PAIRS[k]
            lower_ref[i, r, :, j, :] = total[k - low, :SLAB, :BASIS]
    for copy in back:
        copy.wait_recv()
    for k, (r, i, j) in enumerate(PAIRS):
        upper_ref[j, r, :, i, :] = wide(up_recv[k])[:SLAB, :BASIS]
    copies.finish()


def shards(coeffs, offsets, moments, centers, near_flags, lobe_weights, near_boost):
    pieces, headings, places = grid_tables()
    unknowns = coeffs.shape[2]
    bf16, f32 = jnp.bfloat16, jnp.float32
    operands = (
        coeffs,
        jnp.transpose(offsets, (1, 0, 2)),
        jnp.transpose(moments, (1, 0, 2)),
        jnp.transpose(centers),
        near_flags,
        lobe_weights.reshape(1, -1),
        near_boost.reshape(1, -1),
        jnp.asarray(pieces),
        jnp.asarray(headings),
        jnp.asarray(places),
    )
    held = [pltpu.SMEM if k in (3, 4) else pltpu.VMEM for k in range(len(operands))]
    vmem = pl.BlockSpec(memory_space=pltpu.VMEM)
    out = jax.ShapeDtypeStruct((2, ROUND_TOTAL, SLAB, 2, BASIS), f32)
    lower, upper = pl.pallas_call(
        kernel,
        out_shape=(out, out),
        in_specs=[pl.BlockSpec(memory_space=pltpu.HBM)] * len(operands),
        out_specs=(vmem, vmem),
        scratch_shapes=[
            *(space(operand.shape, operand.dtype) for space, operand in zip(held, operands)),
            pltpu.VMEM((LANES, LANES), bf16),
            pltpu.VMEM((2, DEPTH, unknowns), f32),
            pltpu.VMEM((2, LANES, unknowns), bf16),
            pltpu.VMEM((6 * ROWS, unknowns), f32),
            pltpu.VMEM((2, RING, ROWS, unknowns), bf16),
            pltpu.VMEM((RING, 2, 2, RING, 2, ROWS, 128), bf16),
            pltpu.VMEM((4, 2, 2, 2, ROWS, 128), bf16),
            pltpu.VMEM((4, 2, RING, 2, ROWS, 128), bf16),
            pltpu.VMEM((4, RING, 2, ROWS, 128), bf16),
            pltpu.VMEM((4, 2, ROWS, 128), bf16),
            pltpu.VMEM((4, 2, 2, ROWS, 128), bf16),
            pltpu.VMEM((2, 2, HOLD, LANES), f32),
            pltpu.VMEM((2, RING, 2, HOLD, LANES), bf16),
            pltpu.VMEM((2, RING, HOLD, 2 * HOLD), bf16),
            pltpu.VMEM((ROUND_TOTAL, 2, RING, HOLD, 2 * HOLD), bf16),
            pltpu.VMEM((2, 8, 128), f32),
            pltpu.VMEM((RING, 2, 8, 128), f32),
            pltpu.VMEM((RING, 8, 16, LANES), bf16),
            pltpu.VMEM((RING - 1, 8, 16, LANES), bf16),
            pltpu.VMEM((8, 16, LANES), bf16),
            pltpu.VMEM((8, 16, LANES), bf16),
            pltpu.SemaphoreType.DMA((N_COPIES,)),
            pltpu.SemaphoreType.DMA((N_COPIES,)),
            pltpu.SemaphoreType.DMA((len(operands),)),
        ],
        compiler_params=pltpu.CompilerParams(
            collective_id=0, has_side_effects=True, vmem_limit_bytes=62 * 1024 * 1024
        ),
        name="fill",
    )(*operands)
    return jnp.transpose(lower, (0, 1, 3, 4, 2)), jnp.transpose(upper, (0, 1, 3, 2, 4))


def solution(mesh):
    placed = (
        P("grp", None, "sub"),
        P("grp", None, "sub"),
        P("grp", None, "sub"),
        P(),
        P(),
        P("sub"),
        P("sub"),
    )
    return jax.shard_map(
        shards,
        mesh=mesh,
        in_specs=placed,
        out_specs=(P("grp", None, None, None, "sub"), P("grp", None, None, "sub", None)),
        check_vma=False,
    )
```

time: 87.5 us -> 72.6 us (0.83)
  the two profiles are of different devices: /device:TPU:16 before, /device:TPU:6 now
where the time goes in v2:
time: 72.6 us; the launch traced here: 71.7 us
  Pallas kernels  68.8 us (95%)
  local copies, waits for them, and re-layouts  2.25 us (3%)
    pallas_call x1, Pallas kernels, shards(): pl.pallas_call(kernel, out_shape=(out, out), in_specs=[pl.BlockSpec(memor...  68.8 us
    unnamed x4, local copies, waits for them, and re-layouts  2.25 us

profile of v2, /device:TPU:6, one launch (start us, length us, event | category | flops | bytes accessed | tf_op | source)
XLA Modules:
  0.0 71.7 jit_solution(16874966763693510528)
XLA Ops:
  0.6 68.8 %fill.1 = (f32[2,2,15,2,240]{4,3,2,1,0:T(2,128)}, f32[2,2,15,2,240]{4,3,2,1,0:T(2,128)}) custom-call(bf16[2,240,512]{2,1,0:T(8,128)(2,1)} %coeffs_hbm.1, bf16[3,2,512]{2,1,0:T(2,128)(2,1)} %bitcast.9, bf16[3,2,512]{2,1,0:T(2,128)(2,1)} %bitcast.10, f32[3,64]{1,0:T(4,128)} %bitcast.11, s32[64,64]{1,0:T(8,128)} %flags_hbm.1, f32[1,90]{1,0:T(1,128)} %bitcast.12, ...), custom_call_target="tpu_custom_call" | custom-call | tf_op jit(solution)/shard_map/fill/pallas_call | solution.py:494
  69.5 0.0 copy-start
  69.5 1.6 %copy.14 = f32[2,2,2,240,15]{3,2,4,1,0:T(2,128)} copy(f32[2,2,2,240,15]{3,2,4,1,0:T(2,128)} %bitcast.8) | data formatting | bytes 230400
  71.1 0.0 copy-done
  71.1 0.6 copy.15
Async XLA Ops:
  69.5 1.6 %copy-start = (f32[2,2,15,2,240]{4,3,2,1,0:T(2,128)S(1)}, f32[2,2,15,2,240]{4,3,2,1,0:T(2,128)}, u32[]{:S(2)}) copy-start(f32[2,2,15,2,240]{4,3,2,1,0:T(2,128)} %get-tuple-element.5) | copy-start | bytes 345604

commit v3 on v2

--- a/solution.py
+++ b/solution.py
@@ -22,6 +22,9 @@
 LANES = 256
 DEPTH = 32
 MESH = pl.DeviceIdType.MESH
+ZDIRECT = True
+ORDER = 2
+VMEM_MB = 48
 
 
 def heading_of(t):
@@ -106,19 +109,29 @@
         self.send_sems, self.recv_sems = send_sems, recv_sems
         self.all = []
 
-    def start(self, source, target, device):
+    def start(self, source, target, device, arrival=None):
         place = len(self.all)
         copy = pltpu.make_async_remote_copy(
             src_ref=source,
             dst_ref=target,
             send_sem=self.send_sems.at[place],
-            recv_sem=self.recv_sems.at[place],
+            recv_sem=self.recv_sems.at[place] if arrival is None else arrival,
             device_id=device,
             device_id_type=MESH,
         )
         copy.start()
         self.all.append(copy)
         return copy
+
+    def arrive(self, target, arrival, device):
+        pltpu.make_async_remote_copy(
+            src_ref=target,
+            dst_ref=target,
+            send_sem=self.send_sems.at[0],
+            recv_sem=arrival,
+            device_id=device,
+            device_id_type=MESH,
+        ).wait_recv()
 
     def finish(self):
         for copy in self.all:
@@ -158,7 +171,7 @@
 PAIRS = [(0, 0, 0), (1, 0, 0), (0, 0, 1), (0, 1, 0), (0, 1, 1), (1, 0, 1), (1, 1, 0), (1, 1, 1)]
 PARTS = [(0, 2), (2, 5), (5, 8)]
 UPWARD = [[(0, 1), (1, 2)], [(2, 5)], [(5, 8)]]
-N_COPIES = 4 + 4 * 4 + 4 * 4 + 2 * 3 + 2 * 8 + 3 * 3 + 4
+N_COPIES = 4 + 4 * 4 + 4 * 4 + 4 * 3 + 4 * 4 + 3 * 3 + 4
 
 
 def slab_matrix():
@@ -176,9 +189,9 @@
     coeffs_ref, offsets_ref, moments_ref, centers_ref, flags_ref, weights_ref, boost_ref,
     pieces_ref, headings_ref, places_ref,
     slabs, geometry, coeffs_pad, turned, samples, part, x_near, x_far, z_send, z_near, z_far,
-    patterns, plain, turned_send, turned_recv, lobe_pair, lobe_all,
+    left, turned_send, right, lobe_pair, lobe_all,
     zp, z_recv, up_send, up_recv,
-    send_sems, recv_sems, load_sems,
+    send_sems, recv_sems, left_sems, right_sems, lobe_sems, load_sems,
 ):
     group = lax.axis_index("grp")
     groups = lax.axis_size("grp")
@@ -196,13 +209,13 @@
     z_peers = [at(along(z, d), x) for d in range(1, RING)]
     z_pair = at(z + 1 - 2 * z_odd, x)
 
-    def other(shift, d=0):
-        return {"grp": lax.rem(group + shift + groups, groups), "sub": z * RING + along(x, d)}
-
-    plain[:, :, :, ROWS:] = jnp.zeros((2, RING, 2, HOLD - ROWS, LANES), jnp.bfloat16)
+    def other(shift, x_to):
+        return {"grp": lax.rem(group + shift + groups, groups), "sub": z * RING + x_to}
+
+    left[:, :, :, :, ROWS:] = jnp.zeros((2, 2, RING, 2, HOLD - ROWS, 128), jnp.bfloat16)
 
     barrier = pltpu.get_barrier_semaphore()
-    group_peers = [other(shift, d) for shift in (1, -1, 2, -2) for d in range(RING)]
+    group_peers = [other(shift, x_to) for shift in (1, -1, 2, -2) for x_to in range(RING)]
     peers = x_peers + z_peers + group_peers
     for peer in peers:
         pl.semaphore_signal(barrier, inc=1, device_id=peer, device_id_type=MESH)
@@ -232,7 +245,7 @@
     for load in loads[:4]:
         load.wait()
 
-    for block in range(2):
+    def prepare(block):
         geometry[block] = jnp.zeros((DEPTH, geometry.shape[2]), jnp.float32)
         for axis in range(3):
             offset = wide(offsets_ref[axis])[block : block + 1]
@@ -255,8 +268,8 @@
             cosine, sine = turn(turned[pl.ds(low, 16), :])
             for polar in range(2):
                 weight = turned[pl.ds(low + (polar + 1) * 2 * ROWS, 16), :]
-                samples[0, polar * 2 + half, pl.ds(inner, 16), :] = rounded(weight * cosine)
-                samples[1, polar * 2 + half, pl.ds(inner, 16), :] = rounded(weight * sine)
+                samples[polar * 2 + half, 0, pl.ds(inner, 16), :] = rounded(weight * cosine)
+                samples[polar * 2 + half, 1, pl.ds(inner, 16), :] = rounded(weight * sine)
             return carried
 
         lax.fori_loop(0, 6, rows_of, 0)
@@ -267,18 +280,18 @@
             preferred_element_type=jnp.float32,
         )
         for side in range(2):
-            part[owner, block, :, :, side] = rounded(sums[:, side * 128 : side * 128 + 128]).reshape(
-                2, RING, ROWS, 128
+            part[owner, block, side] = rounded(sums[:, side * 128 : side * 128 + 128]).reshape(
+                RING, 2, ROWS, 128
             )
 
     across, after, before = along(x, 2), along(x, 1), along(x, 3)
-    steps = [(b, c) for b in range(2) for c in range(2)]
+    steps = [(block, side) for block in range(2) for side in range(2)]
     x_rings = [
         Ring(
-            copies, x, x_peers[2], x_peers[0], lambda o, b=b, c=c: part.at[o, b, c],
+            copies, x, x_peers[2], x_peers[0], lambda o, b=b, side=side: part.at[o, b, side],
             pl.ds(0, 2), pl.ds(2, 2), x_near.at[k], x_far.at[k],
         )
-        for k, (b, c) in enumerate(steps)
+        for k, (b, side) in enumerate(steps)
     ]
     z_rings = [
         Ring(
@@ -287,20 +300,54 @@
         )
         for k in range(4)
     ]
+    z_direct = {}
 
     def cross(k):
         z_send[k] = rounded(x_rings[k].total())
-        z_rings[k].step_1()
-
-    def keep(k):
-        total = z_rings[k].total()
-        for side in range(2):
-            patterns[k // 2, k % 2, 0:ROWS, side * 128 : side * 128 + 128] = total[side]
-
+        if ZDIRECT:
+            z_direct[k] = [
+                copies.start(z_send.at[k, along(z, d)], z_far.at[k, d - 1], z_peers[d - 1])
+                for d in (2, 1, 3)
+            ]
+        else:
+            z_rings[k].step_1()
+
+    def z_step_2(k):
+        if not ZDIRECT:
+            z_rings[k].step_2()
+
+    def settle(k):
+        block, side = steps[k]
+        if ZDIRECT:
+            for copy in z_direct[k]:
+                copy.wait_recv()
+            total = wide(z_send[k, z])
+            for d in range(1, RING):
+                total = total + wide(z_far[k, d - 1])
+        else:
+            total = z_rings[k].total()
+        pattern = rounded(total)
+        mine = left.at[side, block, x, :, pl.ds(0, ROWS)]
+        mine[...] = pattern
+        for d in range(1, RING):
+            copies.start(mine, mine, x_peers[d - 1], left_sems.at[side, block, x])
+        held = jnp.concatenate([wide(pattern), jnp.zeros((2, HOLD - ROWS, 128), jnp.float32)], axis=1)
+        turned_send[k] = rounded(jnp.transpose(held.reshape(2 * HOLD, 128))).reshape(2, HOLD, 2 * HOLD)
+        for r in range(ROUND_TOTAL):
+            for e in range(2):
+                copies.start(
+                    turned_send.at[k, e],
+                    right.at[r, block, x],
+                    other(r + 1, 2 * side + e),
+                    right_sems.at[r, block, x],
+                )
+
+    prepare(0)
     project(across, 0)
     pl.semaphore_wait(barrier, len(peers))
     x_rings[0].step_1()
     x_rings[1].step_1()
+    prepare(1)
     project(across, 1)
     x_rings[2].step_1()
     x_rings[3].step_1()
@@ -322,43 +369,20 @@
     x_rings[3].step_2()
     project(x, 0)
     project(x, 1)
-    paired.wait_recv()
-    lobe_all[0] = lobe_pair[...]
-    lobes = [copies.start(lobe_all.at[0], lobe_all.at[d], x_peers[d - 1]) for d in range(1, RING)]
-    patterns[...] = jnp.zeros_like(patterns)
     cross(0)
     cross(1)
-    z_rings[0].step_2()
+    z_step_2(0)
     cross(2)
-    z_rings[1].step_2()
+    z_step_2(1)
     cross(3)
-    z_rings[2].step_2()
-
-    gathered = {}
-
-    def settle(block):
-        pattern = rounded(patterns[block])
-        turned_send[block] = rounded(jnp.transpose(wide(pattern).reshape(2 * HOLD, LANES))).reshape(
-            RING, HOLD, 2 * HOLD
-        )
-        for r in range(ROUND_TOTAL):
-            for d in range(RING):
-                gathered[block, r, d] = copies.start(
-                    turned_send.at[block, along(x, d)], turned_recv.at[r, block, d], other(r + 1, d)
-                )
-        rows = pl.ds(0, ROWS)
-        plain[block, 0, :, rows] = rounded(
-            jnp.dot(pattern.reshape(2 * HOLD, LANES), slabs[...], preferred_element_type=jnp.float32)
-        ).reshape(2, HOLD, LANES)[:, :ROWS]
-        for d in range(1, RING):
-            gathered[block, d] = copies.start(
-                plain.at[block, 0, :, rows], plain.at[block, d, :, rows], x_peers[d - 1]
-            )
-
-    keep(0)
-    keep(1)
+    paired.wait_recv()
+    lobe_all[x] = lobe_pair[...]
+    for d in range(1, RING):
+        copies.start(lobe_all.at[x], lobe_all.at[x], x_peers[d - 1], lobe_sems.at[x])
+    z_step_2(2)
     settle(0)
-    z_rings[3].step_2()
+    z_step_2(3)
+    settle(1)
 
     for load in loads[6:]:
         load.wait()
@@ -375,15 +399,14 @@
     odd = z_odd.astype(jnp.float32)
     below = lax.broadcasted_iota(jnp.int32, (128, 128), 0)
     sign = jnp.where(lax.broadcasted_iota(jnp.int32, (8, 128), 1) < HOLD, 1.0, -1.0)
-    for lobe in lobes:
-        lobe.wait_recv()
+    for d in range(1, RING):
+        there = along(x, d)
+        copies.arrive(lobe_all.at[there], lobe_sems.at[there], x_peers[d - 1])
     cosines, sines = [], []
-    for d in range(RING):
-        source = lax.rem(x - d + RING, RING)
-        facing = lax.rem(2 * x - d - 3 + 2 * RING, RING)
+    for source in range(RING):
+        near = lobe_all[source, 0] * (1.0 - odd) + lobe_all[source, 1] * odd
+        far = lobe_all[3 - source, 1] * (1.0 - odd) + lobe_all[3 - source, 0] * odd
         table = source * 2 + z_odd
-        near = lobe_all[d, 0] * (1.0 - odd) + lobe_all[d, 1] * odd
-        far = lobe_all[facing, 1] * (1.0 - odd) + lobe_all[facing, 0] * odd
         place = places_ref[table]
         sums = jnp.dot(
             near, jnp.where(below == place[0:1], 1.0, 0.0),
@@ -401,28 +424,40 @@
     def couple(k):
         r, i, j = PAIRS[k]
         carries = []
-        for d in range(RING):
-            right = wide(turned_recv[r, j, d])
+        for source in range(RING):
+            value = wide(right[r, j, source])
             carries.append(
                 rounded(
-                    cosines[d][k : k + 1] * right + sines[d][k : k + 1] * pltpu.roll(right, HOLD, 1)
+                    cosines[source][k : k + 1] * value
+                    + sines[source][k : k + 1] * pltpu.roll(value, HOLD, 1)
                 )
             )
-        total = jnp.dot(
-            jnp.concatenate(carries, axis=1),
-            plain[i].reshape(RING * 2 * HOLD, LANES),
-            preferred_element_type=jnp.float32,
-        )
+        carry = jnp.concatenate(carries, axis=1)
+        total = jnp.concatenate(
+            [
+                jnp.dot(
+                    carry, left[side, i].reshape(RING * 2 * HOLD, 128), preferred_element_type=jnp.float32
+                )
+                for side in range(2)
+            ],
+            axis=1,
+        )
+        total = jnp.dot(rounded(total), slabs[...], preferred_element_type=jnp.float32)
         zp[:, k] = rounded(total).reshape(RING, 16, LANES)
 
-    def arrived(block, rounds):
-        for r in rounds:
-            for d in range(RING):
-                gathered[block, r, d].wait_recv()
-
-    def arrived_own(block):
-        for d in range(1, RING):
-            gathered[block, d].wait_recv()
+    def arrived_right(r, block):
+        for source in range(RING):
+            copies.arrive(right.at[r, block, source], right_sems.at[r, block, source], other(-r - 1, source))
+
+    def arrived_left(block):
+        for side in range(2):
+            for d in range(1, RING):
+                there = along(x, d)
+                copies.arrive(
+                    left.at[side, block, there, :, pl.ds(0, ROWS)],
+                    left_sems.at[side, block, there],
+                    x_peers[d - 1],
+                )
 
     spread = []
 
@@ -438,16 +473,28 @@
             ]
         )
 
-    arrived(0, [0, 1])
-    arrived_own(0)
-    scatter(0)
-    keep(2)
-    keep(3)
-    settle(1)
-    arrived(1, [0])
-    arrived_own(1)
+    def early():
+        arrived_left(0)
+        arrived_right(0, 0)
+        arrived_right(1, 0)
+        scatter(0)
+
+    if ORDER == 0:
+        early()
+        settle(2)
+        settle(3)
+    elif ORDER == 1:
+        settle(2)
+        early()
+        settle(3)
+    else:
+        settle(2)
+        settle(3)
+        early()
+    arrived_left(1)
+    arrived_right(0, 1)
     scatter(1)
-    arrived(1, [1])
+    arrived_right(1, 1)
     scatter(2)
 
     back = []
@@ -461,7 +508,7 @@
         up_send[pairs] = rounded(total)
         for first, last in UPWARD[p]:
             mine = pl.ds(first, last - first)
-            back.append(copies.start(up_send.at[mine], up_recv.at[mine], other(-PAIRS[first][0] - 1)))
+            back.append(copies.start(up_send.at[mine], up_recv.at[mine], other(-PAIRS[first][0] - 1, x)))
         for k in range(low, high):
             r, i, j = PAIRS[k]
             lower_ref[i, r, :, j, :] = total[k - low, :SLAB, :BASIS]
@@ -490,7 +537,7 @@
     )
     held = [pltpu.SMEM if k in (3, 4) else pltpu.VMEM for k in range(len(operands))]
     vmem = pl.BlockSpec(memory_space=pltpu.VMEM)
-    out = jax.ShapeDtypeStruct((2, ROUND_TOTAL, SLAB, 2, BASIS), f32)
+    out = pltpu.VMEM((2, ROUND_TOTAL, SLAB, 2, BASIS), f32)
     lower, upper = pl.pallas_call(
         kernel,
         out_shape=(out, out),
@@ -502,16 +549,15 @@
             pltpu.VMEM((2, DEPTH, unknowns), f32),
             pltpu.VMEM((2, LANES, unknowns), bf16),
             pltpu.VMEM((6 * ROWS, unknowns), f32),
-            pltpu.VMEM((2, RING, ROWS, unknowns), bf16),
+            pltpu.VMEM((RING, 2, ROWS, unknowns), bf16),
             pltpu.VMEM((RING, 2, 2, RING, 2, ROWS, 128), bf16),
             pltpu.VMEM((4, 2, 2, 2, ROWS, 128), bf16),
             pltpu.VMEM((4, 2, RING, 2, ROWS, 128), bf16),
             pltpu.VMEM((4, RING, 2, ROWS, 128), bf16),
             pltpu.VMEM((4, 2, ROWS, 128), bf16),
-            pltpu.VMEM((4, 2, 2, ROWS, 128), bf16),
-            pltpu.VMEM((2, 2, HOLD, LANES), f32),
-            pltpu.VMEM((2, RING, 2, HOLD, LANES), bf16),
-            pltpu.VMEM((2, RING, HOLD, 2 * HOLD), bf16),
+            pltpu.VMEM((4, RING - 1, 2, ROWS, 128), bf16),
+            pltpu.VMEM((2, 2, RING, 2, HOLD, 128), bf16),
+            pltpu.VMEM((4, 2, HOLD, 2 * HOLD), bf16),
             pltpu.VMEM((ROUND_TOTAL, 2, RING, HOLD, 2 * HOLD), bf16),
             pltpu.VMEM((2, 8, 128), f32),
             pltpu.VMEM((RING, 2, 8, 128), f32),
@@ -521,13 +567,16 @@
             pltpu.VMEM((8, 16, LANES), bf16),
             pltpu.SemaphoreType.DMA((N_COPIES,)),
             pltpu.SemaphoreType.DMA((N_COPIES,)),
+            pltpu.SemaphoreType.DMA((2, 2, RING)),
+            pltpu.SemaphoreType.DMA((ROUND_TOTAL, 2, RING)),
+            pltpu.SemaphoreType.DMA((RING,)),
             pltpu.SemaphoreType.DMA((len(operands),)),
         ],
         compiler_params=pltpu.CompilerParams(
-            collective_id=0, has_side_effects=True, vmem_limit_bytes=62 * 1024 * 1024
+            collective_id=0, has_side_effects=True, vmem_limit_bytes=VMEM_MB * 1024 * 1024
         ),
         name="fill",
-    )(*operands)
+    )(*(pltpu.with_memory_space_constraint(operand, pltpu.HBM) for operand in operands))
     return jnp.transpose(lower, (0, 1, 3, 4, 2)), jnp.transpose(upper, (0, 1, 3, 2, 4))
 
 

time: 72.6 us -> 70 us (0.964)
  Pallas kernels: 68.8 us -> 67.3 us
  local copies, waits for them, and re-layouts: 2.25 us -> 1.3 us
    pallas_call x1, Pallas kernels: 68.8 us -> 67.3 us  [shards(): pl.pallas_call(kernel, out_shape=(out, out), in_specs=[pl.BlockSpec(memor...]
    unnamed x4 -> x2, local copies, waits for them, and re-layouts: 2.25 us -> 1.3 us
where the time goes in v3:
time: 70 us; the launch traced here: 69.2 us
  Pallas kernels  67.3 us (96%)
  local copies, waits for them, and re-layouts  1.3 us (2%)
    pallas_call x1, Pallas kernels, shards(): pl.pallas_call(kernel, out_shape=(out, out), in_specs=[pl.BlockSpec(memor...  67.3 us

profile of v3, /device:TPU:6, one launch (start us, length us, event | category | flops | bytes accessed | tf_op | source)
XLA Modules:
  0.0 69.2 jit_solution(24411470331326387)
XLA Ops:
  0.6 67.3 %fill.1 = (f32[2,2,15,2,240]{4,3,2,1,0:T(2,128)S(1)}, f32[2,2,15,2,240]{4,3,2,1,0:T(2,128)S(1)}) custom-call(bf16[2,240,512]{2,1,0:T(8,128)(2,1)} %coeffs_hbm.1, bf16[3,2,512]{2,1,0:T(2,128)(2,1)} %bitcast.9, bf16[3,2,512]{2,1,0:T(2,128)(2,1)} %bitcast.10, f32[3,64]{1,0:T(4,128)} %bitcast.11, s32[64,64]{1,0:T(8,128)} %flags_hbm.1, f32[1,90]{1,0:T(1,128)} %bitcast.12, ...), custom_call_target="tpu_custom_call" | custom-call | tf_op jit(solution)/shard_map/fill/pallas_call | solution.py:541
  67.9 0.7 copy.14
  68.6 0.6 copy.15

commit v4 on v3

--- a/solution.py
+++ b/solution.py
@@ -22,9 +22,9 @@
 LANES = 256
 DEPTH = 32
 MESH = pl.DeviceIdType.MESH
-ZDIRECT = True
-ORDER = 2
-VMEM_MB = 48
+ZRING = True
+PRIO = True
+CENTER = 2
 
 
 def heading_of(t):
@@ -191,7 +191,7 @@
     slabs, geometry, coeffs_pad, turned, samples, part, x_near, x_far, z_send, z_near, z_far,
     left, turned_send, right, lobe_pair, lobe_all,
     zp, z_recv, up_send, up_recv,
-    send_sems, recv_sems, left_sems, right_sems, lobe_sems, load_sems,
+    send_sems, recv_sems, left_sems, right_sems, lobe_sems, z_sems, load_sems, z_in, larger_in, smaller_in,
 ):
     group = lax.axis_index("grp")
     groups = lax.axis_size("grp")
@@ -215,10 +215,60 @@
     left[:, :, :, :, ROWS:] = jnp.zeros((2, 2, RING, 2, HOLD - ROWS, 128), jnp.bfloat16)
 
     barrier = pltpu.get_barrier_semaphore()
-    group_peers = [other(shift, x_to) for shift in (1, -1, 2, -2) for x_to in range(RING)]
-    peers = x_peers + z_peers + group_peers
-    for peer in peers:
+
+    shifts = [(1, lax.rem(group + 1, groups)), (2, lax.rem(group + 2, groups))]
+    shifts += [(-1, lax.rem(group + groups - 1, groups)), (-2, lax.rem(group + groups - 2, groups))]
+    for peer in x_peers:
         pl.semaphore_signal(barrier, inc=1, device_id=peer, device_id_type=MESH)
+
+    @pl.when(z != CENTER)
+    def _():
+        pl.semaphore_signal(barrier, inc=1, device_id=at(CENTER, x), device_id_type=MESH)
+
+    smaller = 0
+    for shift, place in shifts:
+        smaller = smaller + jnp.where(place < group, 1, 0)
+
+        @pl.when(group < place)
+        def _(shift=shift):
+            pl.semaphore_signal(barrier, inc=1, device_id=other(shift, x), device_id_type=MESH)
+
+    greetings = RING - 1 + smaller + jnp.where(z == CENTER, RING - 1, 0)
+
+    def enter():
+        pl.semaphore_wait(barrier, greetings)
+
+        @pl.when(z == CENTER)
+        def _():
+            for peer in z_peers:
+                pl.semaphore_signal(z_in, inc=1, device_id=peer, device_id_type=MESH)
+
+        for shift, place in shifts:
+
+            @pl.when(place < group)
+            def _(shift=shift):
+                pl.semaphore_signal(larger_in, inc=1, device_id=other(shift, x), device_id_type=MESH)
+
+    def enter_z():
+        @pl.when(z != CENTER)
+        def _():
+            pl.semaphore_wait(z_in, 1)
+
+    def enter_larger():
+        @pl.when(smaller < 4)
+        def _():
+            pl.semaphore_wait(larger_in, 4 - smaller)
+
+        for shift, place in shifts:
+
+            @pl.when(group < place)
+            def _(shift=shift):
+                pl.semaphore_signal(smaller_in, inc=1, device_id=other(shift, x), device_id_type=MESH)
+
+    def enter_smaller():
+        @pl.when(smaller > 0)
+        def _():
+            pl.semaphore_wait(smaller_in, smaller)
 
     loads = [
         pltpu.make_async_copy(source, target, load_sems.at[k])
@@ -304,28 +354,23 @@
 
     def cross(k):
         z_send[k] = rounded(x_rings[k].total())
-        if ZDIRECT:
-            z_direct[k] = [
-                copies.start(z_send.at[k, along(z, d)], z_far.at[k, d - 1], z_peers[d - 1])
-                for d in (2, 1, 3)
-            ]
-        else:
+        if ZRING:
             z_rings[k].step_1()
-
-    def z_step_2(k):
-        if not ZDIRECT:
-            z_rings[k].step_2()
+            return
+        z_direct[k] = [
+            copies.start(z_send.at[k, along(z, d)], z_far.at[k, d - 1], z_peers[d - 1]) for d in (2, 1, 3)
+        ]
 
     def settle(k):
         block, side = steps[k]
-        if ZDIRECT:
+        if ZRING:
+            total = z_rings[k].total()
+        else:
             for copy in z_direct[k]:
                 copy.wait_recv()
             total = wide(z_send[k, z])
             for d in range(1, RING):
                 total = total + wide(z_far[k, d - 1])
-        else:
-            total = z_rings[k].total()
         pattern = rounded(total)
         mine = left.at[side, block, x, :, pl.ds(0, ROWS)]
         mine[...] = pattern
@@ -344,7 +389,7 @@
 
     prepare(0)
     project(across, 0)
-    pl.semaphore_wait(barrier, len(peers))
+    enter()
     x_rings[0].step_1()
     x_rings[1].step_1()
     prepare(1)
@@ -357,7 +402,6 @@
     lobe_pair[0] = jnp.zeros((8, 128), jnp.float32)
     lobe_pair[0, 0:1, 0 : weights_ref.shape[1]] = weights_ref[...]
     lobe_pair[0, 1:2, 0 : weights_ref.shape[1]] = boost_ref[...]
-    paired = copies.start(lobe_pair.at[0], lobe_pair.at[1], z_pair)
 
     project(after, 0)
     project(before, 0)
@@ -369,19 +413,27 @@
     x_rings[3].step_2()
     project(x, 0)
     project(x, 1)
+    enter_z()
+    paired = copies.start(lobe_pair.at[0], lobe_pair.at[1], z_pair)
     cross(0)
+    enter_larger()
     cross(1)
-    z_step_2(0)
     cross(2)
-    z_step_2(1)
+    if ZRING:
+        z_rings[0].step_2()
     cross(3)
+    if ZRING:
+        z_rings[1].step_2()
     paired.wait_recv()
     lobe_all[x] = lobe_pair[...]
     for d in range(1, RING):
         copies.start(lobe_all.at[x], lobe_all.at[x], x_peers[d - 1], lobe_sems.at[x])
-    z_step_2(2)
+    if ZRING:
+        z_rings[2].step_2()
+    enter_smaller()
     settle(0)
-    z_step_2(3)
+    if ZRING:
+        z_rings[3].step_2()
     settle(1)
 
     for load in loads[6:]:
@@ -459,52 +511,34 @@
                     x_peers[d - 1],
                 )
 
-    spread = []
-
-    def scatter(p):
-        low, high = PARTS[p]
-        for k in range(low, high):
-            couple(k)
-        pairs = pl.ds(low, high - low)
-        spread.append(
-            [
-                copies.start(zp.at[along(z, d), pairs], z_recv.at[d - 1, pairs], z_peers[d - 1])
-                for d in range(1, RING)
-            ]
-        )
-
-    def early():
-        arrived_left(0)
-        arrived_right(0, 0)
-        arrived_right(1, 0)
-        scatter(0)
-
-    if ORDER == 0:
-        early()
-        settle(2)
-        settle(3)
-    elif ORDER == 1:
-        settle(2)
-        early()
-        settle(3)
-    else:
-        settle(2)
-        settle(3)
-        early()
+    def scatter(parts):
+        for p in parts:
+            for k in range(*PARTS[p]):
+                couple(k)
+        for to_z in [1 - (z + 3) // 4, 3 - 2 * (z // 2), 2 + (z // 2) * (1 - z_odd)] if PRIO else [along(z, d) for d in (1,2,3)]:
+            for p in parts:
+                pairs = pl.ds(PARTS[p][0], PARTS[p][1] - PARTS[p][0])
+                copies.start(zp.at[to_z, pairs], z_recv.at[z, pairs], at(to_z, x), z_sems.at[p, z])
+
+    settle(2)
+    settle(3)
+    arrived_left(0)
+    arrived_right(0, 0)
+    arrived_right(1, 0)
+    scatter([0])
     arrived_left(1)
     arrived_right(0, 1)
-    scatter(1)
     arrived_right(1, 1)
-    scatter(2)
+    scatter([1, 2])
 
     back = []
     for p, (low, high) in enumerate(PARTS):
-        for copy in spread[p]:
-            copy.wait_recv()
         pairs = pl.ds(low, high - low)
         total = wide(zp[z, pairs])
         for d in range(1, RING):
-            total = total + wide(z_recv[d - 1, pairs])
+            there = along(z, d)
+            copies.arrive(z_recv.at[there, pairs], z_sems.at[p, there], z_peers[d - 1])
+            total = total + wide(z_recv[there, pairs])
         up_send[pairs] = rounded(total)
         for first, last in UPWARD[p]:
             mine = pl.ds(first, last - first)
@@ -562,7 +596,7 @@
             pltpu.VMEM((2, 8, 128), f32),
             pltpu.VMEM((RING, 2, 8, 128), f32),
             pltpu.VMEM((RING, 8, 16, LANES), bf16),
-            pltpu.VMEM((RING - 1, 8, 16, LANES), bf16),
+            pltpu.VMEM((RING, 8, 16, LANES), bf16),
             pltpu.VMEM((8, 16, LANES), bf16),
             pltpu.VMEM((8, 16, LANES), bf16),
             pltpu.SemaphoreType.DMA((N_COPIES,)),
@@ -570,10 +604,14 @@
             pltpu.SemaphoreType.DMA((2, 2, RING)),
             pltpu.SemaphoreType.DMA((ROUND_TOTAL, 2, RING)),
             pltpu.SemaphoreType.DMA((RING,)),
+            pltpu.SemaphoreType.DMA((len(PARTS), RING)),
             pltpu.SemaphoreType.DMA((len(operands),)),
+            pltpu.SemaphoreType.REGULAR,
+            pltpu.SemaphoreType.REGULAR,
+            pltpu.SemaphoreType.REGULAR,
         ],
         compiler_params=pltpu.CompilerParams(
-            collective_id=0, has_side_effects=True, vmem_limit_bytes=VMEM_MB * 1024 * 1024
+            collective_id=0, has_side_effects=True, vmem_limit_bytes=48 * 1024 * 1024
         ),
         name="fill",
     )(*(pltpu.with_memory_space_constraint(operand, pltpu.HBM) for operand in operands))

time: 70 us -> 66.4 us (0.949)
  Pallas kernels: 67.3 us -> 64.3 us
    pallas_call x1, Pallas kernels: 67.3 us -> 64.3 us  [shards(): pl.pallas_call(kernel, out_shape=(out, out), in_specs=[pl.BlockSpec(memor...]
where the time goes in v4:
time: 66.4 us; the launch traced here: 66.2 us
  Pallas kernels  64.3 us (97%)
  local copies, waits for them, and re-layouts  1.3 us (2%)
    pallas_call x1, Pallas kernels, shards(): pl.pallas_call(kernel, out_shape=(out, out), in_specs=[pl.BlockSpec(memor...  64.3 us

profile of v4, /device:TPU:6, one launch (start us, length us, event | category | flops | bytes accessed | tf_op | source)
XLA Modules:
  0.0 66.2 jit_solution(10225712180846258493)
XLA Ops:
  0.6 64.3 %fill.1 = (f32[2,2,15,2,240]{4,3,2,1,0:T(2,128)S(1)}, f32[2,2,15,2,240]{4,3,2,1,0:T(2,128)S(1)}) custom-call(bf16[2,240,512]{2,1,0:T(8,128)(2,1)} %coeffs_hbm.1, bf16[3,2,512]{2,1,0:T(2,128)(2,1)} %bitcast.9, bf16[3,2,512]{2,1,0:T(2,128)(2,1)} %bitcast.10, f32[3,64]{1,0:T(4,128)} %bitcast.11, s32[64,64]{1,0:T(8,128)} %flags_hbm.1, f32[1,90]{1,0:T(1,128)} %bitcast.12, ...), custom_call_target="tpu_custom_call" | custom-call | tf_op jit(solution)/shard_map/fill/pallas_call | solution.py:575
  64.9 0.7 copy.14
  65.6 0.6 copy.15

commit v5 on v4

--- a/solution.py
+++ b/solution.py
@@ -22,8 +22,6 @@
 LANES = 256
 DEPTH = 32
 MESH = pl.DeviceIdType.MESH
-ZRING = True
-PRIO = True
 CENTER = 2
 
 
@@ -185,7 +183,7 @@
 def kernel(
     coeffs_hbm, offsets_hbm, moments_hbm, centers_hbm, flags_hbm, weights_hbm, boost_hbm,
     pieces_hbm, headings_hbm, places_hbm,
-    lower_ref, upper_ref,
+    both_ref,
     coeffs_ref, offsets_ref, moments_ref, centers_ref, flags_ref, weights_ref, boost_ref,
     pieces_ref, headings_ref, places_ref,
     slabs, geometry, coeffs_pad, turned, samples, part, x_near, x_far, z_send, z_near, z_far,
@@ -350,28 +348,14 @@
         )
         for k in range(4)
     ]
-    z_direct = {}
 
     def cross(k):
         z_send[k] = rounded(x_rings[k].total())
-        if ZRING:
-            z_rings[k].step_1()
-            return
-        z_direct[k] = [
-            copies.start(z_send.at[k, along(z, d)], z_far.at[k, d - 1], z_peers[d - 1]) for d in (2, 1, 3)
-        ]
+        z_rings[k].step_1()
 
     def settle(k):
         block, side = steps[k]
-        if ZRING:
-            total = z_rings[k].total()
-        else:
-            for copy in z_direct[k]:
-                copy.wait_recv()
-            total = wide(z_send[k, z])
-            for d in range(1, RING):
-                total = total + wide(z_far[k, d - 1])
-        pattern = rounded(total)
+        pattern = rounded(z_rings[k].total())
         mine = left.at[side, block, x, :, pl.ds(0, ROWS)]
         mine[...] = pattern
         for d in range(1, RING):
@@ -419,21 +403,17 @@
     enter_larger()
     cross(1)
     cross(2)
-    if ZRING:
-        z_rings[0].step_2()
+    z_rings[0].step_2()
     cross(3)
-    if ZRING:
-        z_rings[1].step_2()
+    z_rings[1].step_2()
     paired.wait_recv()
     lobe_all[x] = lobe_pair[...]
     for d in range(1, RING):
         copies.start(lobe_all.at[x], lobe_all.at[x], x_peers[d - 1], lobe_sems.at[x])
-    if ZRING:
-        z_rings[2].step_2()
+    z_rings[2].step_2()
     enter_smaller()
     settle(0)
-    if ZRING:
-        z_rings[3].step_2()
+    z_rings[3].step_2()
     settle(1)
 
     for load in loads[6:]:
@@ -515,7 +495,7 @@
         for p in parts:
             for k in range(*PARTS[p]):
                 couple(k)
-        for to_z in [1 - (z + 3) // 4, 3 - 2 * (z // 2), 2 + (z // 2) * (1 - z_odd)] if PRIO else [along(z, d) for d in (1,2,3)]:
+        for to_z in (1 - (z + 3) // 4, 3 - 2 * (z // 2), 2 + (z // 2) * (1 - z_odd)):
             for p in parts:
                 pairs = pl.ds(PARTS[p][0], PARTS[p][1] - PARTS[p][0])
                 copies.start(zp.at[to_z, pairs], z_recv.at[z, pairs], at(to_z, x), z_sems.at[p, z])
@@ -545,11 +525,11 @@
             back.append(copies.start(up_send.at[mine], up_recv.at[mine], other(-PAIRS[first][0] - 1, x)))
         for k in range(low, high):
             r, i, j = PAIRS[k]
-            lower_ref[i, r, :, j, :] = total[k - low, :SLAB, :BASIS]
+            both_ref[0, i, r, :, j, :] = total[k - low, :SLAB, :BASIS]
     for copy in back:
         copy.wait_recv()
     for k, (r, i, j) in enumerate(PAIRS):
-        upper_ref[j, r, :, i, :] = wide(up_recv[k])[:SLAB, :BASIS]
+        both_ref[1, j, r, :, i, :] = wide(up_recv[k])[:SLAB, :BASIS]
     copies.finish()
 
 
@@ -571,12 +551,12 @@
     )
     held = [pltpu.SMEM if k in (3, 4) else pltpu.VMEM for k in range(len(operands))]
     vmem = pl.BlockSpec(memory_space=pltpu.VMEM)
-    out = pltpu.VMEM((2, ROUND_TOTAL, SLAB, 2, BASIS), f32)
-    lower, upper = pl.pallas_call(
+    out = pltpu.VMEM((2, 2, ROUND_TOTAL, SLAB, 2, BASIS), f32)
+    both = pl.pallas_call(
         kernel,
-        out_shape=(out, out),
+        out_shape=out,
         in_specs=[pl.BlockSpec(memory_space=pltpu.HBM)] * len(operands),
-        out_specs=(vmem, vmem),
+        out_specs=vmem,
         scratch_shapes=[
             *(space(operand.shape, operand.dtype) for space, operand in zip(held, operands)),
             pltpu.VMEM((LANES, LANES), bf16),
@@ -589,7 +569,7 @@
             pltpu.VMEM((4, 2, RING, 2, ROWS, 128), bf16),
             pltpu.VMEM((4, RING, 2, ROWS, 128), bf16),
             pltpu.VMEM((4, 2, ROWS, 128), bf16),
-            pltpu.VMEM((4, RING - 1, 2, ROWS, 128), bf16),
+            pltpu.VMEM((4, 2, 2, ROWS, 128), bf16),
             pltpu.VMEM((2, 2, RING, 2, HOLD, 128), bf16),
             pltpu.VMEM((4, 2, HOLD, 2 * HOLD), bf16),
             pltpu.VMEM((ROUND_TOTAL, 2, RING, HOLD, 2 * HOLD), bf16),
@@ -615,6 +595,7 @@
         ),
         name="fill",
     )(*(pltpu.with_memory_space_constraint(operand, pltpu.HBM) for operand in operands))
+    lower, upper = both[0], both[1]
     return jnp.transpose(lower, (0, 1, 3, 4, 2)), jnp.transpose(upper, (0, 1, 3, 2, 4))
 
 

time: 66.4 us -> 65.7 us (0.989)
    unnamed x2 -> x0, local copies, waits for them, and re-layouts: 1.3 us -> none
    transpose x0 -> x1, local copies, waits for them, and re-layouts: none -> 0.71 us  [shards(): jnp.transpose(upper, (0, 1, 3, 2, 4))]
where the time goes in v5:
time: 65.7 us; the launch traced here: 65.6 us
  Pallas kernels  64.2 us (98%)
  local copies, waits for them, and re-layouts  0.71 us (1%)
    pallas_call x1, Pallas kernels, shards(): pl.pallas_call(kernel, out_shape=out, in_specs=[pl.BlockSpec(memory_space...  64.2 us

profile of v5, /device:TPU:6, one launch (start us, length us, event | category | flops | bytes accessed | tf_op | source)
XLA Modules:
  0.0 65.6 jit_solution(10891709480384522311)
XLA Ops:
  0.6 64.2 %fill.1 = f32[2,2,2,15,2,240]{5,4,3,2,1,0:T(2,128)S(1)} custom-call(bf16[2,240,512]{2,1,0:T(8,128)(2,1)} %coeffs_hbm.1, bf16[3,2,512]{2,1,0:T(2,128)(2,1)} %bitcast.13, bf16[3,2,512]{2,1,0:T(2,128)(2,1)} %bitcast.14, f32[3,64]{1,0:T(4,128)} %bitcast.15, s32[64,64]{1,0:T(8,128)} %flags_hbm.1, f32[1,90]{1,0:T(1,128)} %bitcast.16, f32[1,90]{1,0:T(1,128)} %bitcast.17, ...), custom_call_target="tpu_custom_call" | custom-call | tf_op jit(solution)/shard_map/fill/pallas_call | solution.py:555
  64.8 0.7 %slice_bitcast_fusion = (f32[2,2,2,15,240]{4,2,3,1,0:T(2,128)}, f32[2,2,2,240,15]{3,2,4,1,0:T(2,128)}) fusion(f32[2,2,2,15,2,240]{5,4,3,2,1,0:T(2,128)S(1)} %fill.1), kind=kLoop, calls=%fused_computation | loop fusion | bytes 460800 | tf_op jit(solution)/shard_map/transpose | solution.py:599

commit v6 on v5

--- a/solution.py
+++ b/solution.py
@@ -389,10 +389,10 @@
 
     project(after, 0)
     project(before, 0)
+    project(after, 1)
+    project(before, 1)
     x_rings[0].step_2()
     x_rings[1].step_2()
-    project(after, 1)
-    project(before, 1)
     x_rings[2].step_2()
     x_rings[3].step_2()
     project(x, 0)

time: 65.7 us -> 65.2 us (level)
  no operation moved by 1% of the time
where the time goes in v6:
time: 65.2 us; the launch traced here: 65.1 us
  Pallas kernels  63.8 us (98%)
  local copies, waits for them, and re-layouts  0.71 us (1%)
    pallas_call x1, Pallas kernels, shards(): pl.pallas_call(kernel, out_shape=out, in_specs=[pl.BlockSpec(memory_space...  63.8 us

profile of v6, /device:TPU:6, one launch (start us, length us, event | category | flops | bytes accessed | tf_op | source)
XLA Modules:
  0.0 65.1 jit_solution(16832133181001896671)
XLA Ops:
  0.6 63.8 %fill.1 = f32[2,2,2,15,2,240]{5,4,3,2,1,0:T(2,128)S(1)} custom-call(bf16[2,240,512]{2,1,0:T(8,128)(2,1)} %coeffs_hbm.1, bf16[3,2,512]{2,1,0:T(2,128)(2,1)} %bitcast.13, bf16[3,2,512]{2,1,0:T(2,128)(2,1)} %bitcast.14, f32[3,64]{1,0:T(4,128)} %bitcast.15, s32[64,64]{1,0:T(8,128)} %flags_hbm.1, f32[1,90]{1,0:T(1,128)} %bitcast.16, f32[1,90]{1,0:T(1,128)} %bitcast.17, ...), custom_call_target="tpu_custom_call" | custom-call | tf_op jit(solution)/shard_map/fill/pallas_call | solution.py:555
  64.4 0.7 %slice_bitcast_fusion = (f32[2,2,2,15,240]{4,2,3,1,0:T(2,128)}, f32[2,2,2,240,15]{3,2,4,1,0:T(2,128)}) fusion(f32[2,2,2,15,2,240]{5,4,3,2,1,0:T(2,128)S(1)} %fill.1), kind=kLoop, calls=%fused_computation | loop fusion | bytes 460800 | tf_op jit(solution)/shard_map/transpose | solution.py:599
